TPU v7x, 32 devices: a whole 2x2x4 slice. The times are simulated.
32 devices in a mesh: groups: 2 (over x), section: 2 (over core), zero: 8 (over z, y).
Axes of the slice: x: 2, y: 2, z: 4, core: 2. Of those that a mesh axis runs over, the one named last changes fastest.
Arguments:
- inputs: bfloat16 [2048, 8192], P(('groups', 'zero')), parts along dimension 0, may hold values from -6 to 6
- cotangent: bfloat16 [2048, 8192], P(('groups', 'zero')), parts along dimension 0, may hold values from -6 to 6
- weights: bfloat16 [2, 3, 128, 2, 4096], P('section', None, 'zero'), may hold values from -0.75 to 0.75
- keep: int32 [2, 3, 128, 2], P('section', None, 'zero'), may hold values from 0 to 1, as said below
- columns: int32 [2, 3, 128, 2], P('section'), may hold values from 0 to 171, as said below
Outputs:
- outputs: bfloat16 [2, 2048, 8192], P('section', ('groups', 'zero')), parts along dimension 1
- grad_input: bfloat16 [2, 2048, 8192], P('section', ('groups', 'zero')), parts along dimension 1
- grad_weight: float32 [2, 3, 256, 2, 4096], P('section', None, ('groups', 'zero')), parts along dimension 2
There are 2 independent parts, one for each index of `groups`. A program takes and returns all parts, laid end to end along the dimension named above; an argument that names none is the same for every part. Nothing has to cross between parts.
Inputs may be any that keep to these rules, and one draw needn't show every extreme that they name: In every layer and every matrix the 32 slots of the rows held by one device of zero (16 block rows) keep between 8 and 32, and the rows of some device keep all 32. The 2 columns of one block row of one matrix are different.
All inputs are finite; a program needn't handle non-finite values.
Results may differ from a plain program's by a relative error of at most 0.01.
Values may be sent and summed in bfloat16 or wider, within the bound.
A program may use at most 192 MiB of HBM per device.

v0:
```python
import math

import jax
import jax.numpy as jnp
from jax import lax
from jax.sharding import PartitionSpec as P

FF = 11008
BLK = 64


epsilon = 1e-05


def from_behind(value, axis, by):
    size = lax.axis_size(axis)
    pairs = [(i, i + by) for i in range(size) if 0 <= i + by < size]
    return lax.ppermute(value, axis, pairs)


def spread_in(rows_in, block_set, column_set):
    count = rows_in.shape[0]
    row_blocks, slots = column_set.shape
    col_blocks = FF // BLK
    shaped_in = rows_in.reshape(count, row_blocks, BLK)
    shaped_w = block_set.reshape(row_blocks, slots, BLK, BLK)
    parts = jnp.einsum("trb,rkbe->trke", shaped_in, shaped_w, preferred_element_type=jnp.float32)
    placed = jnp.zeros((count, col_blocks, BLK), jnp.float32)
    placed = placed.at[:, column_set.reshape(-1)].add(parts.reshape(count, row_blocks * slots, BLK))
    return placed.reshape(count, col_blocks * BLK)


def pick_columns(hidden_in, column_set):
    count = hidden_in.shape[0]
    row_blocks, slots = column_set.shape
    picked = hidden_in.reshape(count, FF // BLK, BLK)[:, column_set.reshape(-1)]
    return picked.reshape(count, row_blocks, slots, BLK)


def gather_out(hidden_in, block_set, column_set):
    count = hidden_in.shape[0]
    row_blocks, slots = column_set.shape
    picked = pick_columns(hidden_in, column_set)
    shaped_w = block_set.reshape(row_blocks, slots, BLK, BLK)
    out = jnp.einsum("trkj,rkij->tri", picked, shaped_w, preferred_element_type=jnp.float32)
    return out.reshape(count, row_blocks * BLK)


def block_terms(left, right, column_set):
    count = left.shape[0]
    row_blocks, slots = column_set.shape
    rows_in = left.reshape(count, row_blocks, BLK)
    picked = pick_columns(right, column_set)
    terms = jnp.einsum("tri,trkj->rkij", rows_in, picked, preferred_element_type=jnp.float32)
    return terms.reshape(row_blocks, slots, BLK * BLK)


def norm_front(layer_in):
    widened = layer_in.astype(jnp.float32)
    reciprocal = lax.rsqrt(jnp.mean(widened * widened, axis=-1, keepdims=True) + epsilon)
    scaled = widened * reciprocal
    normed = scaled.astype(jnp.bfloat16)
    return (widened, reciprocal, scaled, normed)


def forward_layer(layer_in, blocks, column_sets):
    widened, reciprocal, scaled, normed = norm_front(layer_in)
    pre_gate = spread_in(normed, blocks[0], column_sets[0])
    pre_up = spread_in(normed, blocks[1], column_sets[1])
    hidden = (jax.nn.silu(pre_gate) * pre_up).astype(jnp.bfloat16)
    returned = gather_out(hidden, blocks[2], column_sets[2])
    return ((widened + returned).astype(jnp.bfloat16), pre_gate, pre_up)


def backward_layer(layer_in, pre_gate, pre_up, upstream, blocks, column_sets):
    widened, reciprocal, scaled, normed = norm_front(layer_in)
    logistic = jax.nn.sigmoid(pre_gate)
    silu_gate = pre_gate * logistic
    hidden = (silu_gate * pre_up).astype(jnp.bfloat16)
    grad_hidden = spread_in(upstream, blocks[2], column_sets[2])
    grad_gate = (grad_hidden * pre_up * logistic * (1.0 + pre_gate * (1.0 - logistic))).astype(
        jnp.bfloat16
    )
    grad_up = (grad_hidden * silu_gate).astype(jnp.bfloat16)
    grad_normed = gather_out(grad_gate, blocks[0], column_sets[0]) + gather_out(
        grad_up, blocks[1], column_sets[1]
    )
    inner = jnp.mean(grad_normed * scaled, axis=-1, keepdims=True)
    grad_in = (upstream.astype(jnp.float32) + reciprocal * (grad_normed - scaled * inner)).astype(
        jnp.bfloat16
    )
    terms = jnp.stack(
        [
            block_terms(normed, grad_gate, column_sets[0]),
            block_terms(normed, grad_up, column_sets[1]),
            block_terms(upstream, hidden, column_sets[2]),
        ]
    )
    return (grad_in, terms)


def shards(inputs, cotangent, weights, keep, columns):
    sections = lax.axis_size("section")
    section_id = lax.axis_index("section")
    local_rows, width = inputs.shape
    total_tokens = local_rows * lax.axis_size("zero")
    norm_factor = 1.0 / math.sqrt(total_tokens)
    column_sets = columns[0]
    own_keep = keep[0]
    own_blocks = weights[0] * own_keep[..., None].astype(jnp.bfloat16)
    matrices = lax.all_gather(own_blocks, "zero", axis=1, tiled=True)
    current = inputs
    hidden_zeros = jnp.zeros((local_rows, FF), jnp.float32)
    held = (jnp.zeros_like(inputs), jnp.zeros_like(inputs), hidden_zeros, hidden_zeros)
    for tick in range(sections):

        def advance(layer_in):
            result, pre_gate, pre_up = forward_layer(layer_in, matrices, column_sets)
            return (result, layer_in, pre_gate, pre_up)

        def holding(layer_in, kept_values=held):
            return kept_values

        held = lax.cond(section_id == tick, advance, holding, current)
        if tick + 1 < sections:
            current = from_behind(held[0], "section", 1)
    out_keep, in_keep, gate_keep, up_keep = held
    back_matrices = lax.all_gather(own_blocks, "zero", axis=1, tiled=True)
    upstream = cotangent
    grad_keep = jnp.zeros_like(inputs)
    weight_keep = jnp.zeros(back_matrices.shape, jnp.float32)
    for tick in range(sections - 1, -1, -1):

        def retreat(grad_out):
            return backward_layer(in_keep, gate_keep, up_keep, grad_out, back_matrices, column_sets)

        def resting(grad_out, kept_values=(grad_keep, weight_keep)):
            return kept_values

        grad_keep, weight_keep = lax.cond(section_id == tick, retreat, resting, upstream)
        if tick > 0:
            upstream = from_behind(grad_keep, "section", -1)
    summed = lax.psum_scatter(
        weight_keep.astype(jnp.bfloat16), "zero", scatter_dimension=1, tiled=True
    ).astype(jnp.float32)
    own_grad = summed * own_keep[..., None].astype(jnp.float32) * norm_factor
    return (out_keep[None], grad_keep[None], own_grad[None])


def solution(mesh):
    return jax.shard_map(
        shards,
        mesh=mesh,
        in_specs=(
            P(("groups", "zero"), None),
            P(("groups", "zero"), None),
            P("section", None, "zero", None, None),
            P("section", None, "zero", None),
            P("section", None, None, None),
        ),
        out_specs=(
            P("section", ("groups", "zero"), None),
            P("section", ("groups", "zero"), None),
            P("section", None, ("groups", "zero"), None, None),
        ),
        check_vma=False,
    )
```

profile of v0, /device:TPU:0, one launch (start us, length us, event | category | flops | bytes accessed | tf_op | source)
XLA Modules:
  0.0 1008.5 jit_solution(6621253449827916033)
XLA Ops:
  12.4 101.0 %all-gather.2.cloned.1.call-done = bf16[3,128,2,4096]{3,2,0,1:T(2,128)(2,1)} async-done(((bf16[3,16,2,4096]{3,2,0,1:T(2,128)(2,1)}), bf16[3,128,2,4096]{3,2,0,1:T(2,128)(2,1)}) %all-gather.2.cloned.1.call-update) | async-done | bytes 6291472 | tf_op jit(solution)/shard_map/all_gather | solution.py:111
  113.4 168.9 %conditional.4 = (bf16[128,8192]{0,1:T(8,128)(2,1)}, bf16[128,8192]{0,1:T(8,128)(2,1)}, f32[128,11008]{0,1:T(8,128)}, f32[128,11008]{0,1:T(8,128)}) conditional(s32[]{:T(128)} %convert_element_type.127, () %tuple.45, (bf16[128,8192]{1,0:T(8,128)(2,1)}, s32[3,128,2]{2,1,0:T(8,128)S(1)}, bf16[3,128,2,4096]{3,2,0,1:T(2,128)(2,1)}) %tuple.105), branch_computations={%region_0.0_spmd, %region_1.5_spmd} | conditional | flops 827395456 | bytes 184774720 | solution.py:124
  117.5 16.1 %copy.63 = bf16[3,128,2,4096]{1,3,2,0:T(8,128)(2,1)} copy(bf16[3,128,2,4096]{3,2,0,1:T(2,128)(2,1)} %get-tuple-element.132) | data formatting | bytes 12582912 | tf_op jit(solution)/shard_map
  138.9 7.5 copy.43
  146.5 7.9 copy.42
  167.0 39.4 %scatter_fusion.1 = f32[128,172,64]{0,2,1:T(8,128)} fusion(f32[128,172,64]{0,2,1:T(8,128)} %broadcast.285.clone, s32[256]{0:T(256)S(1)} %bitcast.335, f32[256,128,64]{1,2,0:T(8,128)} %bitcast.265), kind=kCustom, calls=%fused_computation.9 | custom fusion | flops 2097152 | bytes 25166848 | tf_op jit(solution)/shard_map/cond/branch_1_fun/scatter-add | solution.py:29
  206.5 8.9 copy.41
  215.4 6.7 fusion.44
  225.2 39.7 %scatter_fusion = f32[128,172,64]{0,2,1:T(8,128)} fusion(f32[128,172,64]{0,2,1:T(8,128)} %broadcast.285.clone.1, s32[256]{0:T(256)S(1)} %bitcast.336, f32[256,128,64]{1,2,0:T(8,128)} %bitcast.264), kind=kCustom, calls=%fused_computation.8 | custom fusion | flops 2097152 | bytes 25166848 | tf_op jit(solution)/shard_map/cond/branch_1_fun/scatter-add | solution.py:29
  264.9 5.8 multiply_convert_fusion
  287.5 12.3 %conditional.5 = (bf16[128,8192]{0,1:T(8,128)(2,1)}, f32[128,11008]{0,1:T(8,128)}, f32[128,11008]{0,1:T(8,128)}, bf16[1,128,8192]{2,1,0:T(8,128)(2,1)S(1)}) conditional(s32[]{:T(128)} %convert_element_type.126, (bf16[128,8192]{0,1:T(8,128)(2,1)}, bf16[128,8192]{0,1:T(8,128)(2,1)}, f32[128,11008]{0,1:T(8,128)}, ...), branch_computations={%region_5.6_spmd, %region_6.10_spmd} | conditional | flops 830541184 | bytes 176386592 | solution.py:124
  301.2 15.4 %conditional.6 = (bf16[128,8192]{0,1:T(8,128)(2,1)S(1)}, bf16[3,128,2,4096]{1,3,2,0:T(8,128)(2,1)}) conditional(s32[]{:T(128)} %convert_element_type.126, () %tuple.48, (bf16[128,8192]{1,0:T(8,128)(2,1)}, bf16[128,8192]{0,1:T(8,128)(2,1)}, s32[3,128,2]{2,1,0:T(8,128)S(1)}, bf16[3,128,2,4096]{3,2,0,1:T(2,128)(2,1)}, f32[128,11008]{0,1:T(8,128)}, ...), branch_computations={%region_10.11_spmd, %region_11.15_spmd} | conditional | flops 1657968000 | bytes 274310848 | solution.py:140
  317.9 339.0 %collective-permute-done.1 = bf16[128,8192]{0,1:T(8,128)(2,1)S(1)} collective-permute-done((bf16[128,8192]{0,1:T(8,128)(2,1)S(1)}, bf16[128,8192]{0,1:T(8,128)(2,1)S(1)}, u32[]{:S(2)}, u32[]{:S(2)}) %collective-permute-start.1) | collective-permute-done | bytes 2097184 | tf_op jit(solution)/shard_map/ppermute | solution.py:18
  656.9 191.1 %conditional.7 = (bf16[3,128,2,4096]{1,3,2,0:T(8,128)(2,1)}, bf16[1,128,8192]{2,1,0:T(8,128)(2,1)}) conditional(s32[]{:T(128)} %convert_element_type.127, (bf16[3,128,2,4096]{1,3,2,0:T(8,128)(2,1)}, bf16[128,8192]{0,1:T(8,128)(2,1)S(1)}) %tuple.50, (s32[3,128,2]{2,1,0:T(8,128)S(1)}, bf16[3,128,2,4096]{3,2,0,1:T(2,128)(2,1)}, ...), branch_computations={%region_15.16_spmd, %region_16.20_spmd} | conditional | flops 1657968000 | bytes 299476736 | solution.py:140
  657.0 16.4 %copy.67 = bf16[3,128,2,4096]{1,3,2,0:T(8,128)(2,1)} copy(bf16[3,128,2,4096]{3,2,0,1:T(2,128)(2,1)} %get-tuple-element.143) | data formatting | bytes 12582912 | tf_op jit(solution)/shard_map
  679.2 8.9 copy.53
  688.0 6.7 fusion.49
  697.9 39.4 %scatter_fusion.5 = f32[128,172,64]{0,2,1:T(8,128)} fusion(f32[128,172,64]{0,2,1:T(8,128)} %broadcast.302, s32[256]{0:T(256)S(1)} %bitcast.332, f32[256,128,64]{1,2,0:T(8,128)} %bitcast.267), kind=kCustom, calls=%fused_computation.13 | custom fusion | flops 2097152 | bytes 25166848 | tf_op jit(solution)/shard_map/cond/branch_1_fun/scatter-add | solution.py:29
  737.3 9.1 fusion.22
  751.3 6.1 convolution_bitcast_fusion.3
  757.4 8.5 copy.56
  770.9 7.7 copy.57
  781.8 6.9 fusion.50
  788.6 6.5 copy.58
  795.1 5.9 bitcast_add_fusion.2
  815.5 8.8 copy.55
  829.7 8.5 copy.54
  838.2 6.6 pad_maximum_fusion.1
  848.0 16.3 %copy.88 = bf16[3,128,2,4096]{3,2,1,0:T(2,128)(2,1)} copy(bf16[3,128,2,4096]{1,3,2,0:T(8,128)(2,1)} %get-tuple-element.100) | data formatting | bytes 12582912
  864.3 7.3 copy.92
  871.6 9.4 reshape.693
  881.8 115.5 %reduce-scatter.5.cloned.1.call-done = bf16[16,24576]{1,0:T(8,128)(2,1)} async-done(((bf16[128,24576]{1,0:T(8,128)(2,1)}), bf16[16,24576]{1,0:T(8,128)(2,1)}) %reduce-scatter.5.cloned.1.call-update) | async-done | bytes 786448
  (79 shorter events, 105.7 us)
Async XLA Ops:
  7.2 106.2 %all-gather.2.cloned.1.call-start = ((), (), s32[]{:S(2)}) async-start(), calls=%async_computation.1 | async-start | bytes 7077888 | tf_op jit(solution)/shard_map/all_gather | solution.py:111
  11.5 985.8 %reduce-scatter.5.cloned.1.call-start = ((), (), s32[]{:S(2)}) async-start(), calls=%async_computation.2 | async-start | bytes 7077888
  154.4 4.9 copy-start.8
  282.3 5.3 collective-permute-start
  299.8 1.3 copy-start.14
  316.6 340.3 %collective-permute-start.1 = (bf16[128,8192]{0,1:T(8,128)(2,1)S(1)}, bf16[128,8192]{0,1:T(8,128)(2,1)S(1)}, u32[]{:S(2)}, u32[]{:S(2)}) collective-permute-start(bf16[128,8192]{0,1:T(8,128)(2,1)S(1)} %get-tuple-element.98), channel_id=1, source_target_pairs={{8,0},{9,1},{10,2},{11,3},{12,4},{13,5},{14,6},{15,7},{24,16},{25,... | collective-permute-start | bytes 6291464 | tf_op jit(solution)/shard_map/ppermute | solution.py:18
  656.9 31.2 %copy-start.3 = (bf16[128,8192]{0,1:T(8,128)(2,1)}, bf16[128,8192]{0,1:T(8,128)(2,1)S(1)}, u32[]{:S(2)}) copy-start(bf16[128,8192]{0,1:T(8,128)(2,1)S(1)} %get-tuple-element.76) | copy-start | bytes 6291460 | tf_op jit(solution)/shard_map/cond
  781.8 6.9 copy-start.10
  801.0 5.6 copy-start.4
  806.6 5.6 copy-start
  810.9 1.3 copy-start.6
  815.5 8.9 copy-start.7
  838.2 6.6 copy-start.9
  881.0 0.7 copy-start.15
Sparse Core Ops, SparseCore 0:
  11.6 101.7 all-gather.1
  881.1 116.1 reduce-scatter.4
where the time goes:
time: 1020 us; the launch traced here: 1010 us
  waiting for transfers between devices  559 us (55%)
  local copies, waits for them, and re-layouts  195 us (19%)
  other arithmetic  164 us (16%)
  matrix products  50.1 us (5%)
  loops' own time  21.9 us (2%)
  between operations  14.6 us (1%)
    ppermute x2, waiting for transfers between devices, from_behind(): return lax.ppermute(value, axis, pairs)  343 us
    scatter-add x3, other arithmetic, spread_in(): placed.at[:, column_set.reshape(-1)]  119 us
    unnamed x3, waiting for transfers between devices  116 us
    all_gather x1, waiting for transfers between devices, shards(): matrices = lax.all_gather(own_blocks, 'zero', axis=1, tiled=True)  101 us
    another operation x7, local copies, waits for them, and re-layouts  46.5 us
    unnamed x9, local copies, waits for them, and re-layouts  37.5 us
    transpose x3, local copies, waits for them, and re-layouts, block_terms(): jnp.einsum('tri,trkj->rkij', rows_in, picked, preferred_element_type=jnp....  25.8 us
    squeeze x3, local copies, waits for them, and re-layouts, spread_in(): shaped_w = block_set.reshape(row_blocks, slots, BLK, BLK)  25.6 us
  transfers between devices with their start and end apart: 4, of which 4 were waited for; matrix products, arithmetic and copies ran while one was open for 0% of the time, Pallas kernels for 0%

commit v1 on v0

v1 whole, which is shorter than its diff:
```python
import math

import jax
import jax.numpy as jnp
from jax import lax
from jax.experimental import pallas as pl
from jax.experimental.pallas import tpu as pltpu
from jax.sharding import PartitionSpec as P

FF = 11008
BLK = 64
NBC = FF // BLK
BF = jnp.bfloat16
F32 = jnp.float32
epsilon = 1e-05

TN = (((0,), (0,)), ((), ()))
NT = (((1,), (1,)), ((), ()))


def dot(a, b, dims=(((1,), (0,)), ((), ()))):
    return lax.dot_general(a, b, dims, preferred_element_type=F32)


def total_rows(acc):
    return jnp.sum(acc, axis=0, keepdims=True)


def fold(value):
    return jnp.sum(value.reshape(-1, 8, value.shape[-1]), axis=0)


def looped(count, unroll, body):
    def step(i, carry):
        for k in range(unroll):
            body(i * unroll + k)
        return carry

    lax.fori_loop(0, count // unroll, step, 0)


def norm_scale(a_ref):
    rows, blk, tokens = a_ref.shape

    def add(i, acc):
        for k in range(4):
            v = a_ref[i * 4 + k].astype(F32)
            acc = acc + fold(v * v)
        return acc

    acc = lax.fori_loop(0, rows // 4, add, jnp.zeros((8, tokens), F32))
    return lax.rsqrt(total_rows(acc) / (rows * blk) + epsilon)


def column(cols, m, r, k, rows):
    return cols[(m * rows + r) * 2 + k]


def clear(*refs):
    def body(c):
        for ref in refs:
            ref[c] = jnp.zeros(ref.shape[1:], ref.dtype)

    looped(NBC, 4, body)


def spread(cols, m, rows, r, w, x, out):
    res = dot(w, x, TN)
    for k in range(2):
        c = column(cols, m, r, k, rows)
        out[c] += res[k * BLK : (k + 1) * BLK]


def pick(cols, m, rows, r, src):
    return [src[column(cols, m, r, k, rows)] for k in range(2)]


def forward_into(cols, a_ref, w_ref, out_ref, xn, pg, pu, hid, fa=None, fb=None):
    rows = a_ref.shape[0]
    recip = norm_scale(a_ref)

    def normed(r):
        xn[r] = (a_ref[r].astype(F32) * recip).astype(BF)

    looped(rows, 4, normed)
    clear(pg, pu)

    def up(r):
        x = xn[r]
        spread(cols, 0, rows, r, w_ref[0, r], x, pg)
        spread(cols, 1, rows, r, w_ref[1, r], x, pu)

    looped(rows, 4, up)

    def act(c):
        g = pg[c]
        u = pu[c]
        s = 1.0 / (1.0 + jnp.exp(-g))
        silu = g * s
        hid[c] = (silu * u).astype(BF)
        if fa is not None:
            fa[c] = (u * s * (1.0 + g * (1.0 - s))).astype(BF)
            fb[c] = silu.astype(BF)

    looped(NBC, 2, act)

    def down(r):
        o = dot(w_ref[2, r], jnp.concatenate(pick(cols, 2, rows, r, hid), axis=0))
        out_ref[r] = (a_ref[r].astype(F32) + o).astype(BF)

    looped(rows, 4, down)


def backward_into(cols, a_ref, g_ref, w_ref, fa, fb, gh, gg, gu, gn, gin_ref, between=None):
    rows, blk, tokens = a_ref.shape
    recip = norm_scale(a_ref)
    clear(gh)
    looped(rows, 4, lambda r: spread(cols, 2, rows, r, w_ref[2, r], g_ref[r], gh))

    def act(c):
        v = gh[c]
        gg[c] = (v * fa[c].astype(F32)).astype(BF)
        gu[c] = (v * fb[c].astype(F32)).astype(BF)

    looped(NBC, 2, act)

    def back(i, acc):
        for k in range(4):
            r = i * 4 + k
            right = pick(cols, 0, rows, r, gg) + pick(cols, 1, rows, r, gu)
            left = jnp.concatenate([w_ref[0, r], w_ref[1, r]], axis=1)
            v = dot(left, jnp.concatenate(right, axis=0))
            gn[r] = v
            acc = acc + fold(v * (a_ref[r].astype(F32) * recip))
        return acc

    acc = lax.fori_loop(0, rows // 4, back, jnp.zeros((8, tokens), F32))
    inner = total_rows(acc) / (rows * blk)

    def finish(r):
        q = a_ref[r].astype(F32) * recip
        gin_ref[r] = (g_ref[r].astype(F32) + recip * (gn[r] - q * inner)).astype(BF)

    looped(rows, 4, finish)


def first_kernel(cols, a_ref, w_ref, out_ref, xn, pg, pu, hid):
    forward_into(cols, a_ref, w_ref, out_ref, xn, pg, pu, hid)


def middle_kernel(cols, a_ref, g_ref, w_ref, out_ref, gin_ref, fa, fb, hid, xn, pg, pu, gg, gu, gn):
    forward_into(cols, a_ref, w_ref, out_ref, xn, pg, pu, hid, fa, fb)
    backward_into(cols, a_ref, g_ref, w_ref, fa, fb, pg, gg, gu, gn, gin_ref)


def last_kernel(cols, a_ref, g_ref, w_ref, fa, fb, hid, gin_ref, wg_ref, gh, gg, gu, gn):
    rows = a_ref.shape[0]
    backward_into(cols, a_ref, g_ref, w_ref, fa, fb, gh, gg, gu, gn, gin_ref)
    recip = norm_scale(a_ref)

    def terms(r):
        x = (a_ref[r].astype(F32) * recip).astype(BF)
        right = pick(cols, 0, rows, r, gg) + pick(cols, 1, rows, r, gu)
        t = dot(x, jnp.concatenate(right, axis=0), NT).astype(BF)
        wg_ref[0, r] = t[:, : 2 * BLK]
        wg_ref[1, r] = t[:, 2 * BLK :]
        t = dot(g_ref[r], jnp.concatenate(pick(cols, 2, rows, r, hid), axis=0), NT)
        wg_ref[2, r] = t.astype(BF)

    looped(rows, 4, terms)


def call(kernel, cols, arrays, outs, scratch):
    vmem = pl.BlockSpec(memory_space=pltpu.VMEM)
    return pl.pallas_call(
        kernel,
        out_shape=[jax.ShapeDtypeStruct(s, d) for s, d in outs],
        in_specs=[pl.BlockSpec(memory_space=pltpu.SMEM)] + [vmem] * len(arrays),
        out_specs=[vmem] * len(outs),
        scratch_shapes=[pltpu.VMEM(s, d) for s, d in scratch],
        compiler_params=pltpu.CompilerParams(vmem_limit_bytes=58 * 2**20),
    )(cols, *arrays)


def shards(inputs, cotangent, weights, keep, columns):
    sections = lax.axis_size("section")
    section_id = lax.axis_index("section")
    tokens, width = inputs.shape
    rows = width // BLK
    norm_factor = 1.0 / math.sqrt(tokens * lax.axis_size("zero"))
    own_keep = keep[0]
    own_rows = own_keep.shape[1]
    masked = weights[0] * own_keep[..., None].astype(BF)
    own = masked.reshape(3, own_rows, 2, BLK, BLK).transpose(0, 1, 3, 2, 4)
    own = own.reshape(3, own_rows, BLK, 2 * BLK)
    mats = lax.all_gather(own, "zero", axis=1, tiled=True)
    cols = columns[0].reshape(-1)
    tall = (rows, BLK, tokens)
    wide = (NBC, BLK, tokens)
    start = inputs.T.reshape(tall)
    cot = cotangent.T.reshape(tall)
    current = start
    for tick in range(1, sections):
        (out,) = call(
            first_kernel, cols, (current, mats), [(tall, BF)],
            [(tall, BF), (wide, F32), (wide, F32), (wide, BF)],
        )
        moved = lax.ppermute(out, "section", [(i, i + 1) for i in range(sections - 1)])
        current = jnp.where(section_id == 0, start, moved)
    out, gin, fa, fb, hid = call(
        middle_kernel, cols, (current, cot, mats),
        [(tall, BF), (tall, BF), (wide, BF), (wide, BF), (wide, BF)],
        [(tall, BF), (wide, F32), (wide, F32), (wide, BF), (wide, BF), (tall, F32)],
    )
    for tick in range(1, sections):
        moved = lax.ppermute(gin, "section", [(i + 1, i) for i in range(sections - 1)])
        upstream = jnp.where(section_id == sections - 1, cot, moved)
        gin, terms = call(
            last_kernel, cols, (current, upstream, mats, fa, fb, hid),
            [(tall, BF), ((3, rows, BLK, 2 * BLK), BF)],
            [(wide, F32), (wide, BF), (wide, BF), (tall, F32)],
        )
    summed = lax.psum_scatter(terms, "zero", scatter_dimension=1, tiled=True).astype(F32)
    grad = summed.reshape(3, own_rows, BLK, 2, BLK).transpose(0, 1, 3, 2, 4)
    grad = grad.reshape(3, own_rows, 2, BLK * BLK)
    grad = grad * own_keep[..., None].astype(F32) * norm_factor
    flat = (width, tokens)
    return (out.reshape(flat).T[None], gin.reshape(flat).T[None], grad[None])


def solution(mesh):
    return jax.shard_map(
        shards,
        mesh=mesh,
        in_specs=(
            P(("groups", "zero"), None),
            P(("groups", "zero"), None),
            P("section", None, "zero", None, None),
            P("section", None, "zero", None),
            P("section", None, None, None),
        ),
        out_specs=(
            P("section", ("groups", "zero"), None),
            P("section", ("groups", "zero"), None),
            P("section", None, ("groups", "zero"), None, None),
        ),
        check_vma=False,
    )
```

time: 1020 us -> 389 us (0.38); the launches traced: 1010 us -> 388 us
  waiting for transfers between devices: 559 us -> 210 us
  other arithmetic: 164 us -> 10 us
  local copies, waits for them, and re-layouts: 195 us -> 44.4 us
  Pallas kernels: 0 us -> 105 us
  matrix products: 50.1 us -> 0 us
  loops' own time: 21.9 us -> 0 us
    ppermute x2, waiting for transfers between devices: 343 us -> 4.92 us  [the longest x1 4.92 us: shards(): lax.ppermute(gin, 'section', [(i + 1, i) for i in range(sections - 1)])]
    scatter-add x3 -> x0, other arithmetic: 119 us -> none  [spread_in(): placed.at[:, column_set.reshape(-1)]]
    pallas_call x0 -> x3, Pallas kernels: none -> 105 us  [call(): pl.pallas_call(kernel, out_shape=[jax.ShapeDtypeStruct(s, d) for s, d in...]
    another operation x7 -> x1, local copies, waits for them, and re-layouts: 46.5 us -> 0.74 us  [shards(): cols = columns[0].reshape(-1)]
    squeeze x12 -> x1, local copies, waits for them, and re-layouts: 48 us -> 2.98 us  [shards(): masked = weights[0] * own_keep[..., None].astype(BF)]
    dot_general x7 -> x0, matrix products: 38.9 us -> none  [the longest x3 17.5 us: gather_out(): jnp.einsum('trkj,rkij->tri', picked, shaped_w, preferred_element_type=jnp...]
    convert_element_type x6 -> x1, other arithmetic: 25.9 us -> 0.01 us  [shards(): grad = grad * own_keep[..., None].astype(F32) * norm_factor]
    unnamed x9 -> x14, local copies, waits for them, and re-layouts: 37.5 us -> 15.2 us
  transfers between devices with their start and end apart: 4 -> 4, of which waited for: 4 -> 3; matrix products, arithmetic and copies ran while one was open for 0% -> 4% of each run, Pallas kernels for 0% -> 0%
where the time goes in v1:
time: 389 us; the launch traced here: 388 us
  waiting for transfers between devices  210 us (54%)
  Pallas kernels  105 us (27%)
  local copies, waits for them, and re-layouts  44.4 us (11%)
  between operations  14.1 us (4%)
  other arithmetic  10 us (3%)
  starting transfers between devices  4.19 us (1%)
    unnamed x3, waiting for transfers between devices  108 us
    pallas_call x3, Pallas kernels, call(): pl.pallas_call(kernel, out_shape=[jax.ShapeDtypeStruct(s, d) for s, d in...  105 us
    all_gather x1, waiting for transfers between devices, shards(): mats = lax.all_gather(own, 'zero', axis=1, tiled=True)  96.9 us
    unnamed x14, local copies, waits for them, and re-layouts  15.2 us
    reshape x3, local copies, waits for them, and re-layouts, shards(): grad = grad.reshape(3, own_rows, 2, BLK * BLK)  8.55 us
  transfers between devices with their start and end apart: 4, of which 3 were waited for; matrix products, arithmetic and copies ran while one was open for 4% of the time, Pallas kernels for 0%

profile of v1, /device:TPU:0, one launch (start us, length us, event | category | flops | bytes accessed | tf_op | source)
XLA Modules:
  0.0 388.3 jit_solution(3348094169063664087)
XLA Ops:
  7.2 0.0 all-gather.2.cloned.1.call-start
  7.2 3.0 squeeze.3
  10.2 0.1 copy.27
  10.3 1.9 fusion
  12.3 1.5 reshape.63
  13.8 0.0 reduce-scatter.5.cloned.1.call-start
  13.8 0.1 copy.25
  14.0 0.7 reshape_squeeze.3.cols
  14.7 4.1 %copy.26 = bf16[8192,128]{1,0:T(8,128)(2,1)} copy(bf16[8192,128]{0,1:T(8,128)(2,1)} %bitcast.46) | data formatting | bytes 4194304 | tf_op jit(solution)/shard_map/transpose | solution.py:200
  18.8 96.9 %all-gather.2.cloned.1.call-done.w_ref = bf16[3,128,64,128]{3,2,1,0:T(8,128)(2,1)} async-done(((bf16[3,16,64,128]{3,2,1,0:T(8,128)(2,1)}), bf16[3,128,64,128]{3,2,1,0:T(8,128)(2,1)}) %all-gather.2.cloned.1.call-update) | async-done | bytes 6291472 | tf_op jit(solution)/shard_map/all_gather | solution.py:196
  115.6 23.6 %shard_map.76 = bf16[128,64,128]{2,1,0:T(8,128)(2,1)} custom-call(s32[768]{0:T(1024)} %reshape_squeeze.3.cols, bf16[128,64,128]{2,1,0:T(8,128)(2,1)} %bitcast.42, bf16[3,128,64,128]{3,2,1,0:T(8,128)(2,1)} %all-gather.2.cloned.1.call-done.w_ref), custom_call_target="tpu_custom_call" | custom-call | tf_op jit(solution)/shard_map/pallas_call | solution.py:175
  139.2 2.6 collective-permute-start
  141.9 4.3 %copy.29 = bf16[8192,128]{1,0:T(8,128)(2,1)} copy(bf16[8192,128]{0,1:T(8,128)(2,1)} %bitcast.47) | data formatting | bytes 4194304 | tf_op jit(solution)/shard_map/transpose | solution.py:201
  146.1 1.5 broadcast_select_fusion.1.a_ref
  147.7 45.4 %shard_map.77 = (bf16[128,64,128]{2,1,0:T(8,128)(2,1)}, bf16[128,64,128]{2,1,0:T(8,128)(2,1)}, bf16[172,64,128]{2,1,0:T(8,128)(2,1)}, bf16[172,64,128]{2,1,0:T(8,128)(2,1)}, bf16[172,64,128]{2,1,0:T(8,128)(2,1)}) custom-call(s32[768]{0:T(1024)} %reshape_squeeze.3.cols, bf16[128,64,128]{2,1,0:T(8,128)(2,1)} %broadcast_select_fusion.1.a_ref, ...), custom_call_target="tpu_custom_call" | custom-call | tf_op jit(solution)/shard_map/pallas_call | solution.py:175
  193.1 1.5 collective-permute-start.1
  194.6 4.9 %collective-permute-done.1 = bf16[128,64,128]{2,1,0:T(8,128)(2,1)} collective-permute-done((bf16[128,64,128]{2,1,0:T(8,128)(2,1)}, bf16[128,64,128]{2,1,0:T(8,128)(2,1)}, u32[]{:S(2)}, u32[]{:S(2)}) %collective-permute-start.1) | collective-permute-done | bytes 2097184 | tf_op jit(solution)/shard_map/ppermute | solution.py:216
  199.5 3.2 broadcast_select_fusion.g_ref
  202.6 36.4 %shard_map.78 = (bf16[128,64,128]{2,1,0:T(8,128)(2,1)}, bf16[3,128,64,128]{3,2,1,0:T(8,128)(2,1)}) custom-call(s32[768]{0:T(1024)} %reshape_squeeze.3.cols, bf16[128,64,128]{2,1,0:T(8,128)(2,1)} %broadcast_select_fusion.1.a_ref, bf16[128,64,128]{2,1,0:T(8,128)(2,1)} %broadcast_select_fusion.g_ref, ...), custom_call_target="tpu_custom_call" | custom-call | tf_op jit(solution)/shard_map/pallas_call | solution.py:175
  239.0 4.3 %copy.34 = bf16[3,128,64,128]{3,2,0,1:T(8,128)(2,1)S(1)} copy(bf16[3,128,64,128]{3,2,1,0:T(8,128)(2,1)} %get-tuple-element.16) | data formatting | bytes 12582912
  243.3 8.0 %copy.43 = bf16[16,8,192,128]{3,1,2,0:T(8,128)(2,1)} copy(bf16[16,8,192,128]{3,2,1,0:T(8,128)(2,1)S(1)} %bitcast.39) | data formatting | bytes 12582912
  251.4 0.1 copy.33
  251.5 1.5 copy-done.2
  252.9 2.9 copy.30
  255.8 4.1 %copy.31 = bf16[8192,128]{0,1:T(8,128)(2,1)} copy(bf16[8192,128]{1,0:T(8,128)(2,1)} %bitcast.49) | data formatting | bytes 4194304 | tf_op jit(solution)/shard_map/reshape | solution.py:228
  259.9 108.3 %reduce-scatter.5.cloned.1.call-done = bf16[16,24576]{1,0:T(8,128)(2,1)} async-done(((bf16[128,24576]{1,0:T(8,128)(2,1)}), bf16[16,24576]{1,0:T(8,128)(2,1)}) %reduce-scatter.5.cloned.1.call-update) | async-done | bytes 786448
  368.2 1.3 copy.37
  369.5 1.3 copy_convert_fusion
  370.8 3.2 reshape.74
  374.0 2.1 copy.32
  376.1 3.3 reshape.71
  379.4 2.1 multiply_multiply_fusion
  (13 shorter events, 0.1 us)
Async XLA Ops:
  7.2 3.0 copy-start.3
  7.2 108.5 %all-gather.2.cloned.1.call-start = ((), (), s32[]{:S(2)}) async-start(), calls=%async_computation.1 | async-start | bytes 7077888 | tf_op jit(solution)/shard_map/all_gather | solution.py:196
  12.2 1.6 copy-start.4
  13.8 354.4 %reduce-scatter.5.cloned.1.call-start = ((), (), s32[]{:S(2)}) async-start(), calls=%async_computation.2 | async-start | bytes 7077888
  139.2 6.9 %collective-permute-start = (bf16[128,64,128]{2,1,0:T(8,128)(2,1)}, bf16[128,64,128]{2,1,0:T(8,128)(2,1)}, u32[]{:S(2)}, u32[]{:S(2)}) collective-permute-start(bf16[128,64,128]{2,1,0:T(8,128)(2,1)} %shard_map.76), channel_id=1, source_target_pairs={{0,8},{1,9},{2,10},{3,11},{4,12},{5,13},{6,14},{7,15},{16,24},{17,... | collective-permute-start | bytes 6291464 | tf_op jit(solution)/shard_map/ppermute | solution.py:208
  141.9 4.3 %copy-start.1 = (bf16[8192,128]{1,0:T(8,128)(2,1)S(1)}, bf16[8192,128]{1,0:T(8,128)(2,1)}, u32[]{:S(2)}) copy-start(bf16[8192,128]{1,0:T(8,128)(2,1)} %copy.26) | copy-start | bytes 6291460
  147.7 51.8 %copy-start = (bf16[8192,128]{1,0:T(8,128)(2,1)S(1)}, bf16[8192,128]{1,0:T(8,128)(2,1)}, u32[]{:S(2)}) copy-start(bf16[8192,128]{1,0:T(8,128)(2,1)} %copy.29) | copy-start | bytes 6291460
  193.1 6.4 %collective-permute-start.1 = (bf16[128,64,128]{2,1,0:T(8,128)(2,1)}, bf16[128,64,128]{2,1,0:T(8,128)(2,1)}, u32[]{:S(2)}, u32[]{:S(2)}) collective-permute-start(bf16[128,64,128]{2,1,0:T(8,128)(2,1)} %get-tuple-element.11), channel_id=1, source_target_pairs={{8,0},{9,1},{10,2},{11,3},{12,4},{13,5},{14,6},{15,7},{24,16},{25,... | collective-permute-start | bytes 6291464 | tf_op jit(solution)/shard_map/ppermute | solution.py:216
  251.3 1.6 copy-start.2
Sparse Core Ops, SparseCore 0:
  13.9 101.7 all-gather.1
  251.5 116.6 reduce-scatter.4

commit v2 on v1

--- a/solution.py
+++ b/solution.py
@@ -144,18 +144,28 @@
     looped(rows, 4, finish)
 
 
-def first_kernel(cols, a_ref, w_ref, out_ref, xn, pg, pu, hid):
-    forward_into(cols, a_ref, w_ref, out_ref, xn, pg, pu, hid)
-
-
-def middle_kernel(cols, a_ref, g_ref, w_ref, out_ref, gin_ref, fa, fb, hid, xn, pg, pu, gg, gu, gn):
+def first_kernel(cols, sec, a_ref, w_ref, out_ref, xn, pg, pu, hid):
+    @pl.when(sec[0] < sec[1] - 1)
+    def _():
+        forward_into(cols, a_ref, w_ref, out_ref, xn, pg, pu, hid)
+
+
+def middle_kernel(cols, sec, a_ref, g_ref, w_ref, out_ref, gin_ref, fa, fb, hid, xn, pg, pu, ga, gb, gn):
     forward_into(cols, a_ref, w_ref, out_ref, xn, pg, pu, hid, fa, fb)
-    backward_into(cols, a_ref, g_ref, w_ref, fa, fb, pg, gg, gu, gn, gin_ref)
-
-
-def last_kernel(cols, a_ref, g_ref, w_ref, fa, fb, hid, gin_ref, wg_ref, gh, gg, gu, gn):
+
+    @pl.when(sec[0] == sec[1] - 1)
+    def _():
+        backward_into(cols, a_ref, g_ref, w_ref, fa, fb, pg, ga, gb, gn, gin_ref)
+
+        def keep_grads(c):
+            fa[c] = ga[c]
+            fb[c] = gb[c]
+
+        looped(NBC, 4, keep_grads)
+
+
+def terms_into(cols, a_ref, g_ref, gg, gu, hid, wg_ref):
     rows = a_ref.shape[0]
-    backward_into(cols, a_ref, g_ref, w_ref, fa, fb, gh, gg, gu, gn, gin_ref)
     recip = norm_scale(a_ref)
 
     def terms(r):
@@ -170,62 +180,259 @@
     looped(rows, 4, terms)
 
 
-def call(kernel, cols, arrays, outs, scratch):
-    vmem = pl.BlockSpec(memory_space=pltpu.VMEM)
+def last_kernel(cols, sec, a_ref, g_ref, gin_old, w_ref, fa, fb, hid, gin_ref, wg_ref, gh, gg, gu, gn):
+    @pl.when(sec[0] == sec[1] - 1)
+    def _():
+        terms_into(cols, a_ref, g_ref, fa, fb, hid, wg_ref)
+
+        def keep_old(r):
+            gin_ref[r] = gin_old[r]
+
+        looped(a_ref.shape[0], 4, keep_old)
+
+    @pl.when(sec[0] < sec[1] - 1)
+    def _():
+        backward_into(cols, a_ref, g_ref, w_ref, fa, fb, gh, gg, gu, gn, gin_ref)
+        terms_into(cols, a_ref, g_ref, gg, gu, hid, wg_ref)
+
+
+VMEM = pl.BlockSpec(memory_space=pltpu.VMEM)
+ANY = pl.BlockSpec(memory_space=pl.ANY)
+LIMIT = 58 * 2**20
+
+
+def call(kernel, cols, sec, arrays, outs, scratch):
     return pl.pallas_call(
         kernel,
         out_shape=[jax.ShapeDtypeStruct(s, d) for s, d in outs],
-        in_specs=[pl.BlockSpec(memory_space=pltpu.SMEM)] + [vmem] * len(arrays),
-        out_specs=[vmem] * len(outs),
+        in_specs=[pl.BlockSpec(memory_space=pltpu.SMEM)] * 2 + [VMEM] * len(arrays),
+        out_specs=[VMEM] * len(outs),
         scratch_shapes=[pltpu.VMEM(s, d) for s, d in scratch],
-        compiler_params=pltpu.CompilerParams(vmem_limit_bytes=58 * 2**20),
-    )(cols, *arrays)
+        compiler_params=pltpu.CompilerParams(vmem_limit_bytes=LIMIT),
+    )(cols, sec, *arrays)
+
+
+def places(n):
+    half = n // 2
+    me = lax.axis_index("zero")
+    low = lax.rem(me, 2)
+    mine = lax.div(me, 2)
+    return me, me + 1 - 2 * low, half, low, mine
+
+
+def remote(src, dst, send, recv, where):
+    return pltpu.make_async_remote_copy(
+        src_ref=src, dst_ref=dst, send_sem=send, recv_sem=recv,
+        device_id=where, device_id_type=pl.DeviceIdType.MESH,
+    )
+
+
+def greet(targets):
+    barrier = pltpu.get_barrier_semaphore()
+    for t in targets:
+        pl.semaphore_signal(barrier, inc=1, device_id=t, device_id_type=pl.DeviceIdType.MESH)
+    pl.semaphore_wait(barrier, len(targets))
+
+
+def gather_kernel(n, sections, own, x_ref, c_ref, out, xt_ref, ct_ref, local, zs, zr, ys, yr, go):
+    me, partner, half, low, mine = places(n)
+    sec = lax.axis_index("section")
+    other = {"section": sections - 1 - sec}
+    r_own = own.shape[1]
+
+    def peer(d):
+        return lax.rem(mine + d, half) * 2 + low
+
+    def slot(m, who):
+        return out.at[m, pl.ds(who * r_own, r_own)]
+
+    greet([{"zero": peer(d)} for d in range(1, half)] + [{"zero": partner}, other])
+    stays = [pltpu.make_async_copy(own.at[m], slot(m, me), local.at[m]) for m in range(3)]
+    for c in stays:
+        c.start()
+
+    def transposed(p, carry):
+        lanes = pl.ds(pl.multiple_of(p * 2 * BLK, 2 * BLK), 2 * BLK)
+        for src, dst in ((x_ref, xt_ref), (c_ref, ct_ref)):
+            t = src[:, lanes].T
+            dst[2 * p] = t[:BLK]
+            dst[2 * p + 1] = t[BLK:]
+        return carry
+
+    @pl.when(sec == sections - 1)
+    def _():
+        pl.semaphore_wait(go, 1)
+
+    sent = []
+    for m in range(3):
+        for d in range(1, half):
+            c = remote(own.at[m], slot(m, me), zs.at[m, d], zr.at[m, d], {"zero": peer(d)})
+            c.start()
+            sent.append(c)
+        c = remote(own.at[m], slot(m, me), ys.at[m, 0], yr.at[m, 0], {"zero": partner})
+        c.start()
+        sent.append(c)
+    lax.fori_loop(0, x_ref.shape[1] // (2 * BLK), transposed, 0)
+    for m in range(3):
+        for d in range(1, half):
+            who = lax.rem(mine + half - d, half) * 2 + low
+            remote(own.at[m], slot(m, who), zs.at[m, d], zr.at[m, d], {"zero": partner}).wait_recv()
+            c = remote(slot(m, who), slot(m, who), ys.at[m, d], yr.at[m, d], {"zero": partner})
+            c.start()
+            sent.append(c)
+    for m in range(3):
+        for d in range(half):
+            who = lax.rem(mine + half - d, half) * 2 + 1 - low
+            remote(own.at[m], slot(m, who), ys.at[m, d], yr.at[m, d], {"zero": partner}).wait_recv()
+
+    @pl.when(sec == 0)
+    def _():
+        pl.semaphore_signal(go, inc=1, device_id=other, device_id_type=pl.DeviceIdType.MESH)
+
+    for c in sent:
+        c.wait_send()
+    for c in stays:
+        c.wait()
+
+
+def reduce_kernel(n, terms, out_t, gin_t, sums, out_ref, gin_ref, near, mid, far, ys, yr, zs, zr):
+    me, partner, half, low, mine = places(n)
+    r_own = sums.shape[1]
+    greet([{"zero": lax.rem(mine + d, half) * 2 + low} for d in range(1, half)] + [{"zero": partner}])
+    order = list(range(1, half)) + [0]
+    sent = []
+
+    def position(d):
+        return lax.rem(mine + d, half) * 2
+
+    for d in order:
+        for m in range(3):
+            src = terms.at[m, pl.ds((position(d) + 1 - low) * r_own, r_own)]
+            c = remote(src, near.at[d, m], ys.at[d, m], yr.at[d, m], {"zero": partner})
+            c.start()
+            sent.append(c)
+
+    def transposed(p, carry):
+        lanes = pl.ds(pl.multiple_of(p * 2 * BLK, 2 * BLK), 2 * BLK)
+        for src, dst in ((out_t, out_ref), (gin_t, gin_ref)):
+            dst[:, lanes] = jnp.concatenate([src[2 * p], src[2 * p + 1]], axis=0).T
+        return carry
+
+    pairs = out_t.shape[0] // 2
+    todo = len(order)
+    for i, d in enumerate(order):
+        lax.fori_loop(i * pairs // todo, (i + 1) * pairs // todo, transposed, 0)
+        for m in range(3):
+            remote(near.at[d, m], near.at[d, m], ys.at[d, m], yr.at[d, m], {"zero": partner}).wait_recv()
+            first = (position(d) + low) * r_own
+
+            def add(r, carry):
+                both = terms[m, first + r].astype(F32) + near[d, m, r].astype(F32)
+                mid[d, m, r] = both.astype(BF)
+                return carry
+
+            lax.fori_loop(0, r_own, add, 0)
+            if d:
+                c = remote(
+                    mid.at[d, m], far.at[d, m], zs.at[d, m], zr.at[d, m],
+                    {"zero": position(d) + low},
+                )
+                c.start()
+                sent.append(c)
+    for m in range(3):
+        for d in range(1, half):
+            remote(mid.at[d, m], far.at[d, m], zs.at[d, m], zr.at[d, m], {"zero": partner}).wait_recv()
+
+        def total(r, carry):
+            value = mid[0, m, r].astype(F32)
+            for d in range(1, half):
+                value = value + far[d, m, r].astype(F32)
+            sums[m, r] = value
+            return carry
+
+        lax.fori_loop(0, r_own, total, 0)
+    for c in sent:
+        c.wait_send()
+
+
+def gather_all(own, x, c, n, sections):
+    tokens, width = x.shape
+    three, r_own, blk, two = own.shape
+    half = n // 2
+    tall = (width // BLK, BLK, tokens)
+    sems = pltpu.SemaphoreType.DMA((3, half))
+    return pl.pallas_call(
+        lambda *refs: gather_kernel(n, sections, *refs),
+        out_shape=[
+            jax.ShapeDtypeStruct((three, n * r_own, blk, two), BF),
+            jax.ShapeDtypeStruct(tall, BF),
+            jax.ShapeDtypeStruct(tall, BF),
+        ],
+        in_specs=[ANY, VMEM, VMEM],
+        out_specs=[ANY, VMEM, VMEM],
+        scratch_shapes=[pltpu.SemaphoreType.DMA((3,)), sems, sems, sems, sems, pltpu.SemaphoreType.REGULAR],
+        compiler_params=pltpu.CompilerParams(collective_id=0, has_side_effects=True, vmem_limit_bytes=LIMIT),
+    )(own, x, c)
+
+
+def reduce_all(terms, out_t, gin_t, n):
+    three, rows, blk, two = terms.shape
+    half = n // 2
+    r_own = rows // n
+    tokens = out_t.shape[2]
+    flat = jax.ShapeDtypeStruct((tokens, rows * blk), BF)
+    held = pltpu.VMEM((half, 3, r_own, blk, two), BF)
+    sems = pltpu.SemaphoreType.DMA((half, 3))
+    return pl.pallas_call(
+        lambda *refs: reduce_kernel(n, *refs),
+        out_shape=[jax.ShapeDtypeStruct((three, r_own, blk, two), F32), flat, flat],
+        in_specs=[VMEM] * 3,
+        out_specs=[VMEM] * 3,
+        scratch_shapes=[held, held, held, sems, sems, sems, sems],
+        compiler_params=pltpu.CompilerParams(collective_id=1, has_side_effects=True, vmem_limit_bytes=LIMIT),
+    )(terms, out_t, gin_t)
 
 
 def shards(inputs, cotangent, weights, keep, columns):
     sections = lax.axis_size("section")
     section_id = lax.axis_index("section")
+    n = lax.axis_size("zero")
     tokens, width = inputs.shape
     rows = width // BLK
-    norm_factor = 1.0 / math.sqrt(tokens * lax.axis_size("zero"))
+    norm_factor = 1.0 / math.sqrt(tokens * n)
     own_keep = keep[0]
     own_rows = own_keep.shape[1]
     masked = weights[0] * own_keep[..., None].astype(BF)
     own = masked.reshape(3, own_rows, 2, BLK, BLK).transpose(0, 1, 3, 2, 4)
     own = own.reshape(3, own_rows, BLK, 2 * BLK)
-    mats = lax.all_gather(own, "zero", axis=1, tiled=True)
+    mats, start, cot = gather_all(own, inputs, cotangent, n, sections)
     cols = columns[0].reshape(-1)
+    sec = jnp.stack([section_id, jnp.int32(sections)]).astype(jnp.int32)
     tall = (rows, BLK, tokens)
     wide = (NBC, BLK, tokens)
-    start = inputs.T.reshape(tall)
-    cot = cotangent.T.reshape(tall)
-    current = start
-    for tick in range(1, sections):
-        (out,) = call(
-            first_kernel, cols, (current, mats), [(tall, BF)],
-            [(tall, BF), (wide, F32), (wide, F32), (wide, BF)],
-        )
-        moved = lax.ppermute(out, "section", [(i, i + 1) for i in range(sections - 1)])
-        current = jnp.where(section_id == 0, start, moved)
+    (out,) = call(
+        first_kernel, cols, sec, (start, mats), [(tall, BF)],
+        [(tall, BF), (wide, F32), (wide, F32), (wide, BF)],
+    )
+    moved = lax.ppermute(out, "section", [(0, 1)])
+    current = jnp.where(section_id == 0, start, moved)
     out, gin, fa, fb, hid = call(
-        middle_kernel, cols, (current, cot, mats),
+        middle_kernel, cols, sec, (current, cot, mats),
         [(tall, BF), (tall, BF), (wide, BF), (wide, BF), (wide, BF)],
         [(tall, BF), (wide, F32), (wide, F32), (wide, BF), (wide, BF), (tall, F32)],
     )
-    for tick in range(1, sections):
-        moved = lax.ppermute(gin, "section", [(i + 1, i) for i in range(sections - 1)])
-        upstream = jnp.where(section_id == sections - 1, cot, moved)
-        gin, terms = call(
-            last_kernel, cols, (current, upstream, mats, fa, fb, hid),
-            [(tall, BF), ((3, rows, BLK, 2 * BLK), BF)],
-            [(wide, F32), (wide, BF), (wide, BF), (tall, F32)],
-        )
-    summed = lax.psum_scatter(terms, "zero", scatter_dimension=1, tiled=True).astype(F32)
+    moved = lax.ppermute(gin, "section", [(1, 0)])
+    upstream = jnp.where(section_id == sections - 1, cot, moved)
+    gin, terms = call(
+        last_kernel, cols, sec, (current, upstream, gin, mats, fa, fb, hid),
+        [(tall, BF), ((3, rows, BLK, 2 * BLK), BF)],
+        [(wide, F32), (wide, BF), (wide, BF), (tall, F32)],
+    )
+    summed, out, gin = reduce_all(terms, out, gin, n)
     grad = summed.reshape(3, own_rows, BLK, 2, BLK).transpose(0, 1, 3, 2, 4)
     grad = grad.reshape(3, own_rows, 2, BLK * BLK)
     grad = grad * own_keep[..., None].astype(F32) * norm_factor
-    flat = (width, tokens)
-    return (out.reshape(flat).T[None], gin.reshape(flat).T[None], grad[None])
+    return (out[None], gin[None], grad[None])
 
 
 def solution(mesh):

time: 389 us -> 295 us (0.76)
  waiting for transfers between devices: 210 us -> 25.7 us
  Pallas kernels: 105 us -> 214 us
  local copies, waits for them, and re-layouts: 44.4 us -> 17.8 us
  starting transfers between devices: 4.19 us -> 26.8 us
  between operations: 14.1 us -> 0.73 us
    pallas_call x0 -> x2, Pallas kernels: none -> 124 us  [the longest x1 69 us: reduce_all(): pl.pallas_call(lambda *refs: reduce_kernel(n, *refs), out_shape=[jax.Shap...]
    unnamed x3 -> x0, waiting for transfers between devices: 108 us -> none
    all_gather x1 -> x0, waiting for transfers between devices: 96.9 us -> none  [shards(): mats = lax.all_gather(own, 'zero', axis=1, tiled=True)]
    ppermute x2, starting transfers between devices: 4.11 us -> 26.8 us  [the longest x1 25.5 us: shards(): moved = lax.ppermute(out, 'section', [(0, 1)])]
    ppermute x2, waiting for transfers between devices: 4.92 us -> 25.7 us  [the longest x1 22.9 us: shards(): moved = lax.ppermute(gin, 'section', [(1, 0)])]
    pallas_call x3, Pallas kernels: 105 us -> 89.8 us  [call(): pl.pallas_call(kernel, out_shape=[jax.ShapeDtypeStruct(s, d) for s, d in...]
    unnamed x14 -> x13, local copies, waits for them, and re-layouts: 15.2 us -> 3.82 us
    transpose x2 -> x1, local copies, waits for them, and re-layouts: 8.32 us -> 2.06 us  [shards(): grad = summed.reshape(3, own_rows, BLK, 2, BLK).transpose(0, 1, 3, 2, 4)]
  transfers between devices with their start and end apart: 4 -> 2, of which waited for: 3 -> 2; matrix products, arithmetic and copies ran while one was open for 4% -> 0% of each run, Pallas kernels for 0% -> 0%
where the time goes in v2:
time: 295 us
  Pallas kernels  214 us (73%)
  starting transfers between devices  26.8 us (9%)
  waiting for transfers between devices  25.7 us (9%)
  local copies, waits for them, and re-layouts  17.8 us (6%)
  other arithmetic  10.1 us (3%)
    pallas_call x3, Pallas kernels, call(): pl.pallas_call(kernel, out_shape=[jax.ShapeDtypeStruct(s, d) for s, d in...  89.8 us
    pallas_call x1, Pallas kernels, reduce_all(): pl.pallas_call(lambda *refs: reduce_kernel(n, *refs), out_shape=[jax.Shap...  69 us
    pallas_call x1, Pallas kernels, gather_all(): pl.pallas_call(lambda *refs: gather_kernel(n, sections, *refs), out_shape...  54.9 us
    ppermute x1, starting transfers between devices, shards(): moved = lax.ppermute(out, 'section', [(0, 1)])  25.5 us
    ppermute x1, waiting for transfers between devices, shards(): moved = lax.ppermute(gin, 'section', [(1, 0)])  22.9 us
  transfers between devices with their start and end apart: 2, of which 2 were waited for; matrix products, arithmetic and copies ran while one was open for 0% of the time, Pallas kernels for 0%

profile of v2, /device:TPU:0, one launch (start us, length us, event | category | flops | bytes accessed | tf_op | source)
XLA Modules:
  0.0 294.8 jit_solution(653480486430265026)
XLA Ops:
  0.6 0.8 convert_bitcast_fusion
  1.4 0.1 copy.13
  1.5 3.0 %squeeze.3 = bf16[3,16,2,64,64]{4,3,2,1,0:T(8,128)(2,1)S(1)} reshape(bf16[1,3,16,2,4096]{4,3,2,1,0:T(2,128)(2,1)} %param.7) | data formatting | bytes 1572864 | tf_op jit(solution)/shard_map/squeeze | solution.py:405
  4.5 0.0 copy-start.4
  4.5 1.9 fusion
  6.4 1.5 reshape.46.refs_0_
  7.9 0.0 copy-done.4
  7.9 0.1 copy.12
  8.0 0.7 reshape_squeeze.3.cols
  8.8 0.6 pad_add_fusion.sec
  9.4 54.9 %shard_map.76 = (bf16[3,128,64,128]{3,2,1,0:T(8,128)(2,1)}, bf16[128,64,128]{2,1,0:T(8,128)(2,1)}, bf16[128,64,128]{2,1,0:T(8,128)(2,1)}) custom-call(bf16[3,16,64,128]{3,2,1,0:T(8,128)(2,1)} %reshape.46.refs_0_, bf16[128,8192]{1,0:T(8,128)(2,1)} %refs_1_.1, bf16[128,8192]{1,0:T(8,128)(2,1)} %refs_2_.1), custom_call_target="tpu_custom_call" | custom-call | tf_op jit(solution)/shard_map/pallas_call | solution.py:364
  64.3 0.0 copy-start.1
  64.3 23.7 %shard_map.77 = bf16[128,64,128]{2,1,0:T(8,128)(2,1)} custom-call(s32[768]{0:T(1024)} %reshape_squeeze.3.cols, s32[2]{0:T(128)} %pad_add_fusion.sec, bf16[128,64,128]{2,1,0:T(8,128)(2,1)} %get-tuple-element.16.a_ref, bf16[3,128,64,128]{3,2,1,0:T(8,128)(2,1)} %get-tuple-element.17.w_ref), custom_call_target="tpu_custom_call" | custom-call | tf_op jit(solution)/shard_map/pallas_call | solution.py:205
  88.1 25.5 %collective-permute-start = (bf16[128,64,128]{2,1,0:T(8,128)(2,1)}, bf16[128,64,128]{2,1,0:T(8,128)(2,1)}, u32[]{:S(2)}, u32[]{:S(2)}) collective-permute-start(bf16[128,64,128]{2,1,0:T(8,128)(2,1)} %shard_map.77), channel_id=1, source_target_pairs={{0,8},{1,9},{2,10},{3,11},{4,12},{5,13},{6,14},{7,15},{16,24},{17,... | collective-permute-start | bytes 6291464 | tf_op jit(solution)/shard_map/ppermute | solution.py:417
  113.6 2.8 collective-permute-done
  116.3 1.5 broadcast_select_fusion.1.a_ref
  117.9 28.8 %shard_map.78 = (bf16[128,64,128]{2,1,0:T(8,128)(2,1)}, bf16[128,64,128]{2,1,0:T(8,128)(2,1)}, bf16[172,64,128]{2,1,0:T(8,128)(2,1)}, bf16[172,64,128]{2,1,0:T(8,128)(2,1)}, bf16[172,64,128]{2,1,0:T(8,128)(2,1)}) custom-call(s32[768]{0:T(1024)} %reshape_squeeze.3.cols, s32[2]{0:T(128)} %pad_add_fusion.sec, ...), custom_call_target="tpu_custom_call" | custom-call | tf_op jit(solution)/shard_map/pallas_call | solution.py:205
  146.7 1.3 collective-permute-start.1
  148.0 0.1 copy.16
  148.1 22.9 %collective-permute-done.1 = bf16[128,64,128]{2,1,0:T(8,128)(2,1)} collective-permute-done((bf16[128,64,128]{2,1,0:T(8,128)(2,1)}, bf16[128,64,128]{2,1,0:T(8,128)(2,1)}, u32[]{:S(2)}, u32[]{:S(2)}) %collective-permute-start.1) | collective-permute-done | bytes 2097184 | tf_op jit(solution)/shard_map/ppermute | solution.py:424
  171.0 0.0 copy-done
  171.0 3.2 %broadcast_select_fusion.g_ref = bf16[128,64,128]{2,1,0:T(8,128)(2,1)} fusion(bf16[128,64,128]{2,1,0:T(8,128)(2,1)S(1)} %copy-done, bf16[128,64,128]{2,1,0:T(8,128)(2,1)} %collective-permute-done.1, pred[]{:T(512)S(6)} %eq.7), kind=kLoop, calls=%fused_computation | loop fusion | flops 1048576 | bytes 6291457 | tf_op jit(solution)/shard_map/jit(_where)/select_n | solution.py:425
  174.1 37.3 %shard_map.79 = (bf16[128,64,128]{2,1,0:T(8,128)(2,1)}, bf16[3,128,64,128]{3,2,1,0:T(8,128)(2,1)}) custom-call(s32[768]{0:T(1024)} %reshape_squeeze.3.cols, s32[2]{0:T(128)} %pad_add_fusion.sec, bf16[128,64,128]{2,1,0:T(8,128)(2,1)} %broadcast_select_fusion.1.a_ref, bf16[128,64,128]{2,1,0:T(8,128)(2,1)} %broadcast_select_fusion.g_ref, ...), custom_call_target="tpu_custom_call" | custom-call | tf_op jit(solution)/shard_map/pallas_call | solution.py:205
  211.5 69.0 %shard_map.80 = (f32[3,16,64,128]{3,2,1,0:T(8,128)}, bf16[128,8192]{1,0:T(8,128)(2,1)}, bf16[128,8192]{1,0:T(8,128)(2,1)}) custom-call(bf16[3,128,64,128]{3,2,1,0:T(8,128)(2,1)} %get-tuple-element.23.refs_0_, bf16[128,64,128]{2,1,0:T(8,128)(2,1)} %get-tuple-element.24.refs_1_, bf16[128,64,128]{2,1,0:T(8,128)(2,1)} %get-tuple-element.25.refs_2_), custom_call_target="tpu_custom_call" | custom-call | tf_op jit(solution)/shard_map/pallas_call | solution.py:386
  280.5 3.2 %reshape.47 = f32[3,16,64,2,64]{4,3,2,1,0:T(2,128)S(1)} reshape(f32[3,16,64,128]{3,2,1,0:T(8,128)} %get-tuple-element.28) | data formatting | bytes 3145728 | tf_op jit(solution)/shard_map/reshape | solution.py:432
  283.7 2.1 copy.15
  285.8 3.3 %reshape.48 = f32[1,3,16,2,4096]{4,3,2,1,0:T(2,128)S(1)} reshape(f32[3,16,2,64,64]{4,3,2,1,0:T(8,128)} %copy.15) | data formatting | bytes 3145728 | tf_op jit(solution)/shard_map/reshape | solution.py:433
  289.1 2.1 multiply_multiply_fusion
  291.2 0.0 copy-done.3
  291.2 1.3 copy.22
  292.5 1.0 copy-done.2
  293.5 1.3 copy.23
  (4 shorter events, 0.0 us)
Async XLA Ops:
  4.5 3.4 %copy-start.4 = (s32[1,3,128,2]{2,3,1,0:T(2,128)S(1)}, s32[1,3,128,2]{2,3,1,0:T(2,128)}, u32[]{:S(2)}) copy-start(s32[1,3,128,2]{2,3,1,0:T(2,128)} %param.9) | copy-start | bytes 9220
  64.3 52.0 %copy-start.1 = (bf16[128,64,128]{2,1,0:T(8,128)(2,1)S(1)}, bf16[128,64,128]{2,1,0:T(8,128)(2,1)}, u32[]{:S(2)}) copy-start(bf16[128,64,128]{2,1,0:T(8,128)(2,1)} %get-tuple-element.16.a_ref) | copy-start | bytes 6291460
  88.1 28.3 %collective-permute-start = (bf16[128,64,128]{2,1,0:T(8,128)(2,1)}, bf16[128,64,128]{2,1,0:T(8,128)(2,1)}, u32[]{:S(2)}, u32[]{:S(2)}) collective-permute-start(bf16[128,64,128]{2,1,0:T(8,128)(2,1)} %shard_map.77), channel_id=1, source_target_pairs={{0,8},{1,9},{2,10},{3,11},{4,12},{5,13},{6,14},{7,15},{16,24},{17,... | collective-permute-start | bytes 6291464 | tf_op jit(solution)/shard_map/ppermute | solution.py:417
  117.9 53.1 %copy-start = (bf16[128,64,128]{2,1,0:T(8,128)(2,1)S(1)}, bf16[128,64,128]{2,1,0:T(8,128)(2,1)}, u32[]{:S(2)}) copy-start(bf16[128,64,128]{2,1,0:T(8,128)(2,1)} %get-tuple-element.18.g_ref) | copy-start | bytes 6291460
  146.7 24.3 %collective-permute-start.1 = (bf16[128,64,128]{2,1,0:T(8,128)(2,1)}, bf16[128,64,128]{2,1,0:T(8,128)(2,1)}, u32[]{:S(2)}, u32[]{:S(2)}) collective-permute-start(bf16[128,64,128]{2,1,0:T(8,128)(2,1)} %get-tuple-element.19.gin_old), channel_id=1, source_target_pairs={{8,0},{9,1},{10,2},{11,3},{12,4},{13,5},{14,6},{15,7},{24,16},{25,... | collective-permute-start | bytes 6291464 | tf_op jit(solution)/shard_map/ppermute | solution.py:424
  289.1 2.1 copy-start.3
  291.2 2.3 copy-start.2

commit v3 on v2

--- a/solution.py
+++ b/solution.py
@@ -111,9 +111,8 @@
     looped(rows, 4, down)
 
 
-def backward_into(cols, a_ref, g_ref, w_ref, fa, fb, gh, gg, gu, gn, gin_ref, between=None):
-    rows, blk, tokens = a_ref.shape
-    recip = norm_scale(a_ref)
+def spread_back(cols, g_ref, w_ref, fa, fb, gh, gg, gu):
+    rows = g_ref.shape[0]
     clear(gh)
     looped(rows, 4, lambda r: spread(cols, 2, rows, r, w_ref[2, r], g_ref[r], gh))
 
@@ -123,6 +122,10 @@
         gu[c] = (v * fb[c].astype(F32)).astype(BF)
 
     looped(NBC, 2, act)
+
+
+def back_sums(cols, a_ref, recip, w_ref, gg, gu, gn, first, last, acc):
+    rows = a_ref.shape[0]
 
     def back(i, acc):
         for k in range(4):
@@ -134,12 +137,23 @@
             acc = acc + fold(v * (a_ref[r].astype(F32) * recip))
         return acc
 
-    acc = lax.fori_loop(0, rows // 4, back, jnp.zeros((8, tokens), F32))
+    return lax.fori_loop(first // 4, last // 4, back, acc)
+
+
+def grad_rows(a_ref, g_ref, recip, gn, inner, r):
+    q = a_ref[r].astype(F32) * recip
+    return (g_ref[r].astype(F32) + recip * (gn[r] - q * inner)).astype(BF)
+
+
+def backward_into(cols, a_ref, g_ref, w_ref, fa, fb, gh, gg, gu, gn, gin_ref):
+    rows, blk, tokens = a_ref.shape
+    recip = norm_scale(a_ref)
+    spread_back(cols, g_ref, w_ref, fa, fb, gh, gg, gu)
+    acc = back_sums(cols, a_ref, recip, w_ref, gg, gu, gn, 0, rows, jnp.zeros((8, tokens), F32))
     inner = total_rows(acc) / (rows * blk)
 
     def finish(r):
-        q = a_ref[r].astype(F32) * recip
-        gin_ref[r] = (g_ref[r].astype(F32) + recip * (gn[r] - q * inner)).astype(BF)
+        gin_ref[r] = grad_rows(a_ref, g_ref, recip, gn, inner, r)
 
     looped(rows, 4, finish)
 
@@ -164,36 +178,29 @@
         looped(NBC, 4, keep_grads)
 
 
-def terms_into(cols, a_ref, g_ref, gg, gu, hid, wg_ref):
+def terms_at(cols, a_ref, g_ref, recip, gg, gu, hid, wg_ref, r):
     rows = a_ref.shape[0]
-    recip = norm_scale(a_ref)
-
-    def terms(r):
-        x = (a_ref[r].astype(F32) * recip).astype(BF)
-        right = pick(cols, 0, rows, r, gg) + pick(cols, 1, rows, r, gu)
-        t = dot(x, jnp.concatenate(right, axis=0), NT).astype(BF)
-        wg_ref[0, r] = t[:, : 2 * BLK]
-        wg_ref[1, r] = t[:, 2 * BLK :]
-        t = dot(g_ref[r], jnp.concatenate(pick(cols, 2, rows, r, hid), axis=0), NT)
-        wg_ref[2, r] = t.astype(BF)
-
-    looped(rows, 4, terms)
-
-
-def last_kernel(cols, sec, a_ref, g_ref, gin_old, w_ref, fa, fb, hid, gin_ref, wg_ref, gh, gg, gu, gn):
+    x = (a_ref[r].astype(F32) * recip).astype(BF)
+    right = pick(cols, 0, rows, r, gg) + pick(cols, 1, rows, r, gu)
+    t = dot(x, jnp.concatenate(right, axis=0), NT).astype(BF)
+    wg_ref[0, r] = t[:, : 2 * BLK]
+    wg_ref[1, r] = t[:, 2 * BLK :]
+    t = dot(g_ref[r], jnp.concatenate(pick(cols, 2, rows, r, hid), axis=0), NT)
+    wg_ref[2, r] = t.astype(BF)
+
+
+def last_kernel(cols, sec, g_ref, w_ref, fa, fb, gg, gu, gh):
     @pl.when(sec[0] == sec[1] - 1)
     def _():
-        terms_into(cols, a_ref, g_ref, fa, fb, hid, wg_ref)
-
-        def keep_old(r):
-            gin_ref[r] = gin_old[r]
-
-        looped(a_ref.shape[0], 4, keep_old)
+        def keep(c):
+            gg[c] = fa[c]
+            gu[c] = fb[c]
+
+        looped(NBC, 4, keep)
 
     @pl.when(sec[0] < sec[1] - 1)
     def _():
-        backward_into(cols, a_ref, g_ref, w_ref, fa, fb, gh, gg, gu, gn, gin_ref)
-        terms_into(cols, a_ref, g_ref, gg, gu, hid, wg_ref)
+        spread_back(cols, g_ref, w_ref, fa, fb, gh, gg, gu)
 
 
 VMEM = pl.BlockSpec(memory_space=pltpu.VMEM)
@@ -272,56 +279,74 @@
         c = remote(own.at[m], slot(m, me), ys.at[m, 0], yr.at[m, 0], {"zero": partner})
         c.start()
         sent.append(c)
-    lax.fori_loop(0, x_ref.shape[1] // (2 * BLK), transposed, 0)
+    pairs = x_ref.shape[1] // (2 * BLK)
+    steps = 3 * (half - 1)
     for m in range(3):
         for d in range(1, half):
+            at = m * (half - 1) + d - 1
+            lax.fori_loop(at * pairs // steps, (at + 1) * pairs // steps, transposed, 0)
             who = lax.rem(mine + half - d, half) * 2 + low
             remote(own.at[m], slot(m, who), zs.at[m, d], zr.at[m, d], {"zero": partner}).wait_recv()
             c = remote(slot(m, who), slot(m, who), ys.at[m, d], yr.at[m, d], {"zero": partner})
             c.start()
             sent.append(c)
+
+    @pl.when(sec == 0)
+    def _():
+        pl.semaphore_signal(go, inc=1, device_id=other, device_id_type=pl.DeviceIdType.MESH)
+
     for m in range(3):
         for d in range(half):
             who = lax.rem(mine + half - d, half) * 2 + 1 - low
             remote(own.at[m], slot(m, who), ys.at[m, d], yr.at[m, d], {"zero": partner}).wait_recv()
 
-    @pl.when(sec == 0)
-    def _():
-        pl.semaphore_signal(go, inc=1, device_id=other, device_id_type=pl.DeviceIdType.MESH)
-
     for c in sent:
         c.wait_send()
     for c in stays:
         c.wait()
 
 
-def reduce_kernel(n, terms, out_t, gin_t, sums, out_ref, gin_ref, near, mid, far, ys, yr, zs, zr):
+def reduce_kernel(
+    n, sections, cols, a_ref, g_ref, w_ref, gg, gu, hid, gin_old, out_t, sums, out_ref, gin_ref,
+    terms, gn, part, near, mid, far, ys, yr, zs, zr
+):
     me, partner, half, low, mine = places(n)
+    sec = lax.axis_index("section")
+    rows, blk, tokens = a_ref.shape
     r_own = sums.shape[1]
     greet([{"zero": lax.rem(mine + d, half) * 2 + low} for d in range(1, half)] + [{"zero": partner}])
     order = list(range(1, half)) + [0]
+    todo = len(order)
     sent = []
+    recip = norm_scale(a_ref)
+    part[...] = jnp.zeros_like(part)
 
     def position(d):
         return lax.rem(mine + d, half) * 2
 
+    def block_of(who):
+        def body(r):
+            terms_at(cols, a_ref, g_ref, recip, gg, gu, hid, terms, who * r_own + r)
+
+        looped(r_own, 4, body)
+
     for d in order:
+        who = position(d) + 1 - low
+        block_of(who)
         for m in range(3):
-            src = terms.at[m, pl.ds((position(d) + 1 - low) * r_own, r_own)]
+            src = terms.at[m, pl.ds(who * r_own, r_own)]
             c = remote(src, near.at[d, m], ys.at[d, m], yr.at[d, m], {"zero": partner})
             c.start()
             sent.append(c)
 
-    def transposed(p, carry):
-        lanes = pl.ds(pl.multiple_of(p * 2 * BLK, 2 * BLK), 2 * BLK)
-        for src, dst in ((out_t, out_ref), (gin_t, gin_ref)):
-            dst[:, lanes] = jnp.concatenate([src[2 * p], src[2 * p + 1]], axis=0).T
-        return carry
-
-    pairs = out_t.shape[0] // 2
-    todo = len(order)
     for i, d in enumerate(order):
-        lax.fori_loop(i * pairs // todo, (i + 1) * pairs // todo, transposed, 0)
+        block_of(position(d) + low)
+
+        @pl.when(sec < sections - 1)
+        def _():
+            first, last = (i * rows // todo, (i + 1) * rows // todo)
+            part[...] = back_sums(cols, a_ref, recip, w_ref, gg, gu, gn, first, last, part[...])
+
         for m in range(3):
             remote(near.at[d, m], near.at[d, m], ys.at[d, m], yr.at[d, m], {"zero": partner}).wait_recv()
             first = (position(d) + low) * r_own
@@ -339,6 +364,26 @@
                 )
                 c.start()
                 sent.append(c)
+
+    def flipped(dst, rows_of):
+        def body(p, carry):
+            lanes = pl.ds(pl.multiple_of(p * 2 * BLK, 2 * BLK), 2 * BLK)
+            dst[:, lanes] = jnp.concatenate([rows_of(2 * p), rows_of(2 * p + 1)], axis=0).T
+            return carry
+
+        lax.fori_loop(0, rows // 2, body, 0)
+
+    flipped(out_ref, lambda r: out_t[r])
+
+    @pl.when(sec == sections - 1)
+    def _():
+        flipped(gin_ref, lambda r: gin_old[r])
+
+    @pl.when(sec < sections - 1)
+    def _():
+        inner = total_rows(part[...]) / (rows * blk)
+        flipped(gin_ref, lambda r: grad_rows(a_ref, g_ref, recip, gn, inner, r))
+
     for m in range(3):
         for d in range(1, half):
             remote(mid.at[d, m], far.at[d, m], zs.at[d, m], zr.at[d, m], {"zero": partner}).wait_recv()
@@ -375,22 +420,26 @@
     )(own, x, c)
 
 
-def reduce_all(terms, out_t, gin_t, n):
-    three, rows, blk, two = terms.shape
+def reduce_all(n, sections, own_rows, cols, a, g, mats, gg, gu, hid, gin_old, out_t):
+    three, rows, blk, two = mats.shape
     half = n // 2
-    r_own = rows // n
     tokens = out_t.shape[2]
     flat = jax.ShapeDtypeStruct((tokens, rows * blk), BF)
-    held = pltpu.VMEM((half, 3, r_own, blk, two), BF)
+    held = pltpu.VMEM((half, 3, own_rows, blk, two), BF)
     sems = pltpu.SemaphoreType.DMA((half, 3))
     return pl.pallas_call(
-        lambda *refs: reduce_kernel(n, *refs),
-        out_shape=[jax.ShapeDtypeStruct((three, r_own, blk, two), F32), flat, flat],
-        in_specs=[VMEM] * 3,
+        lambda *refs: reduce_kernel(n, sections, *refs),
+        out_shape=[jax.ShapeDtypeStruct((three, own_rows, blk, two), F32), flat, flat],
+        in_specs=[pl.BlockSpec(memory_space=pltpu.SMEM)] + [VMEM] * 8,
         out_specs=[VMEM] * 3,
-        scratch_shapes=[held, held, held, sems, sems, sems, sems],
+        scratch_shapes=[
+            pltpu.VMEM(mats.shape, BF),
+            pltpu.VMEM((rows, blk, tokens), F32),
+            pltpu.VMEM((8, tokens), F32),
+            held, held, held, sems, sems, sems, sems,
+        ],
         compiler_params=pltpu.CompilerParams(collective_id=1, has_side_effects=True, vmem_limit_bytes=LIMIT),
-    )(terms, out_t, gin_t)
+    )(cols, a, g, mats, gg, gu, hid, gin_old, out_t)
 
 
 def shards(inputs, cotangent, weights, keep, columns):
@@ -423,12 +472,12 @@
     )
     moved = lax.ppermute(gin, "section", [(1, 0)])
     upstream = jnp.where(section_id == sections - 1, cot, moved)
-    gin, terms = call(
-        last_kernel, cols, sec, (current, upstream, gin, mats, fa, fb, hid),
-        [(tall, BF), ((3, rows, BLK, 2 * BLK), BF)],
-        [(wide, F32), (wide, BF), (wide, BF), (tall, F32)],
+    gg, gu = call(
+        last_kernel, cols, sec, (upstream, mats, fa, fb), [(wide, BF), (wide, BF)], [(wide, F32)]
     )
-    summed, out, gin = reduce_all(terms, out, gin, n)
+    summed, out, gin = reduce_all(
+        n, sections, own_rows, cols, current, upstream, mats, gg, gu, hid, gin, out
+    )
     grad = summed.reshape(3, own_rows, BLK, 2, BLK).transpose(0, 1, 3, 2, 4)
     grad = grad.reshape(3, own_rows, 2, BLK * BLK)
     grad = grad * own_keep[..., None].astype(F32) * norm_factor

time: 295 us -> 286 us (0.969)
  starting transfers between devices: 26.8 us -> 11.4 us
  Pallas kernels: 214 us -> 220 us
    pallas_call x3, Pallas kernels: 89.8 us -> 68.9 us  [call(): pl.pallas_call(kernel, out_shape=[jax.ShapeDtypeStruct(s, d) for s, d in...]
    pallas_call x1, Pallas kernels: 69 us -> 88 us  [reduce_all(): pl.pallas_call(lambda *refs: reduce_kernel(n, sections, *refs), out_shape...]
    ppermute x1, starting transfers between devices: 25.5 us -> 10.1 us  [shards(): moved = lax.ppermute(out, 'section', [(0, 1)])]
    pallas_call x1, Pallas kernels: 54.9 us -> 62.8 us  [gather_all(): pl.pallas_call(lambda *refs: gather_kernel(n, sections, *refs), out_shape...]
where the time goes in v3:
time: 286 us; the launch traced here: 285 us
  Pallas kernels  220 us (77%)
  waiting for transfers between devices  25.7 us (9%)
  local copies, waits for them, and re-layouts  17.8 us (6%)
  starting transfers between devices  11.4 us (4%)
  other arithmetic  10.2 us (4%)
    pallas_call x1, Pallas kernels, reduce_all(): pl.pallas_call(lambda *refs: reduce_kernel(n, sections, *refs), out_shape...  88 us
    pallas_call x3, Pallas kernels, call(): pl.pallas_call(kernel, out_shape=[jax.ShapeDtypeStruct(s, d) for s, d in...  68.9 us
    pallas_call x1, Pallas kernels, gather_all(): pl.pallas_call(lambda *refs: gather_kernel(n, sections, *refs), out_shape...  62.8 us
    ppermute x1, waiting for transfers between devices, shards(): moved = lax.ppermute(gin, 'section', [(1, 0)])  22.9 us
    ppermute x1, starting transfers between devices, shards(): moved = lax.ppermute(out, 'section', [(0, 1)])  10.1 us
  transfers between devices with their start and end apart: 2, of which 2 were waited for; matrix products, arithmetic and copies ran while one was open for 0% of the time, Pallas kernels for 0%

profile of v3, /device:TPU:0, one launch (start us, length us, event | category | flops | bytes accessed | tf_op | source)
XLA Modules:
  0.0 285.4 jit_solution(7262428202404448606)
XLA Ops:
  0.6 0.8 convert_bitcast_fusion
  1.4 0.1 copy.13
  1.5 3.0 %squeeze.3 = bf16[3,16,2,64,64]{4,3,2,1,0:T(8,128)(2,1)S(1)} reshape(bf16[1,3,16,2,4096]{4,3,2,1,0:T(2,128)(2,1)} %param.7) | data formatting | bytes 1572864 | tf_op jit(solution)/shard_map/squeeze | solution.py:454
  4.5 0.0 copy-start.4
  4.5 1.9 fusion
  6.4 1.5 reshape.46.refs_0_
  7.9 0.0 copy-done.4
  7.9 0.1 copy.12
  8.0 0.7 reshape_squeeze.3.cols.refs_0_
  8.8 0.7 pad_add_fusion.sec
  9.4 62.8 %shard_map.76 = (bf16[3,128,64,128]{3,2,1,0:T(8,128)(2,1)}, bf16[128,64,128]{2,1,0:T(8,128)(2,1)}, bf16[128,64,128]{2,1,0:T(8,128)(2,1)}) custom-call(bf16[3,16,64,128]{3,2,1,0:T(8,128)(2,1)} %reshape.46.refs_0_, bf16[128,8192]{1,0:T(8,128)(2,1)} %refs_1_.1, bf16[128,8192]{1,0:T(8,128)(2,1)} %refs_2_.1), custom_call_target="tpu_custom_call" | custom-call | tf_op jit(solution)/shard_map/pallas_call | solution.py:409
  72.2 0.0 copy-start.1
  72.3 23.7 %shard_map.77 = bf16[128,64,128]{2,1,0:T(8,128)(2,1)} custom-call(s32[768]{0:T(1024)} %reshape_squeeze.3.cols.refs_0_, s32[2]{0:T(128)} %pad_add_fusion.sec, bf16[128,64,128]{2,1,0:T(8,128)(2,1)} %get-tuple-element.16.a_ref, bf16[3,128,64,128]{3,2,1,0:T(8,128)(2,1)} %get-tuple-element.17.w_ref.refs_3_), custom_call_target="tpu_custom_call" | custom-call | tf_op jit(solution)/shard_map/pallas_call | solution.py:212
  96.0 10.1 %collective-permute-start = (bf16[128,64,128]{2,1,0:T(8,128)(2,1)}, bf16[128,64,128]{2,1,0:T(8,128)(2,1)}, u32[]{:S(2)}, u32[]{:S(2)}) collective-permute-start(bf16[128,64,128]{2,1,0:T(8,128)(2,1)} %shard_map.77), channel_id=1, source_target_pairs={{0,8},{1,9},{2,10},{3,11},{4,12},{5,13},{6,14},{7,15},{16,24},{17,... | collective-permute-start | bytes 6291464 | tf_op jit(solution)/shard_map/ppermute | solution.py:466
  106.1 2.7 collective-permute-done
  108.9 0.0 copy-done.1
  108.9 1.5 broadcast_select_fusion.1.a_ref.refs_1_
  110.4 28.8 %shard_map.78 = (bf16[128,64,128]{2,1,0:T(8,128)(2,1)}, bf16[128,64,128]{2,1,0:T(8,128)(2,1)}, bf16[172,64,128]{2,1,0:T(8,128)(2,1)}, bf16[172,64,128]{2,1,0:T(8,128)(2,1)}, bf16[172,64,128]{2,1,0:T(8,128)(2,1)}) custom-call(s32[768]{0:T(1024)} %reshape_squeeze.3.cols.refs_0_, s32[2]{0:T(128)} %pad_add_fusion.sec, ...), custom_call_target="tpu_custom_call" | custom-call | tf_op jit(solution)/shard_map/pallas_call | solution.py:212
  139.2 1.3 collective-permute-start.1
  140.5 0.1 copy.16
  140.6 22.9 %collective-permute-done.1 = bf16[128,64,128]{2,1,0:T(8,128)(2,1)} collective-permute-done((bf16[128,64,128]{2,1,0:T(8,128)(2,1)}, bf16[128,64,128]{2,1,0:T(8,128)(2,1)}, u32[]{:S(2)}, u32[]{:S(2)}) %collective-permute-start.1) | collective-permute-done | bytes 2097184 | tf_op jit(solution)/shard_map/ppermute | solution.py:473
  163.5 0.0 copy-done
  163.5 3.2 %broadcast_select_fusion.g_ref.refs_2_ = bf16[128,64,128]{2,1,0:T(8,128)(2,1)} fusion(bf16[128,64,128]{2,1,0:T(8,128)(2,1)S(1)} %copy-done, bf16[128,64,128]{2,1,0:T(8,128)(2,1)} %collective-permute-done.1, pred[]{:T(512)S(6)} %eq.7), kind=kLoop, calls=%fused_computation | loop fusion | flops 1048576 | bytes 6291457 | tf_op jit(solution)/shard_map/jit(_where)/select_n | solution.py:474
  166.8 16.4 %shard_map.79 = (bf16[172,64,128]{2,1,0:T(8,128)(2,1)}, bf16[172,64,128]{2,1,0:T(8,128)(2,1)}) custom-call(s32[768]{0:T(1024)} %reshape_squeeze.3.cols.refs_0_, s32[2]{0:T(128)} %pad_add_fusion.sec, bf16[128,64,128]{2,1,0:T(8,128)(2,1)} %broadcast_select_fusion.g_ref.refs_2_, bf16[3,128,64,128]{3,2,1,0:T(8,128)(2,1)} %get-tuple-element.17.w_ref.refs_3_, ...), custom_call_target="tpu_custom_call" | custom-call | tf_op jit(solution)/shard_map/pallas_call | solution.py:212
  183.1 88.0 %shard_map.80 = (f32[3,16,64,128]{3,2,1,0:T(8,128)}, bf16[128,8192]{1,0:T(8,128)(2,1)}, bf16[128,8192]{1,0:T(8,128)(2,1)}) custom-call(s32[768]{0:T(1024)} %reshape_squeeze.3.cols.refs_0_, bf16[128,64,128]{2,1,0:T(8,128)(2,1)} %broadcast_select_fusion.1.a_ref.refs_1_, bf16[128,64,128]{2,1,0:T(8,128)(2,1)} %broadcast_select_fusion.g_ref.refs_2_, ...), custom_call_target="tpu_custom_call" | custom-call | tf_op jit(solution)/shard_map/pallas_call | solution.py:430
  271.1 3.2 %reshape.47 = f32[3,16,64,2,64]{4,3,2,1,0:T(2,128)S(1)} reshape(f32[3,16,64,128]{3,2,1,0:T(8,128)} %get-tuple-element.28) | data formatting | bytes 3145728 | tf_op jit(solution)/shard_map/reshape | solution.py:481
  274.3 2.1 copy.15
  276.4 3.3 %reshape.48 = f32[1,3,16,2,4096]{4,3,2,1,0:T(2,128)S(1)} reshape(f32[3,16,2,64,64]{4,3,2,1,0:T(8,128)} %copy.15) | data formatting | bytes 3145728 | tf_op jit(solution)/shard_map/reshape | solution.py:482
  279.7 2.1 multiply_multiply_fusion
  281.8 1.3 copy.22
  283.1 1.0 copy-done.2
  284.1 1.3 copy.23
  (4 shorter events, 0.0 us)
Async XLA Ops:
  4.5 3.4 %copy-start.4 = (s32[1,3,128,2]{2,3,1,0:T(2,128)S(1)}, s32[1,3,128,2]{2,3,1,0:T(2,128)}, u32[]{:S(2)}) copy-start(s32[1,3,128,2]{2,3,1,0:T(2,128)} %param.9) | copy-start | bytes 9220
  72.2 36.6 %copy-start.1 = (bf16[128,64,128]{2,1,0:T(8,128)(2,1)S(1)}, bf16[128,64,128]{2,1,0:T(8,128)(2,1)}, u32[]{:S(2)}) copy-start(bf16[128,64,128]{2,1,0:T(8,128)(2,1)} %get-tuple-element.16.a_ref) | copy-start | bytes 6291460
  96.0 12.9 %collective-permute-start = (bf16[128,64,128]{2,1,0:T(8,128)(2,1)}, bf16[128,64,128]{2,1,0:T(8,128)(2,1)}, u32[]{:S(2)}, u32[]{:S(2)}) collective-permute-start(bf16[128,64,128]{2,1,0:T(8,128)(2,1)} %shard_map.77), channel_id=1, source_target_pairs={{0,8},{1,9},{2,10},{3,11},{4,12},{5,13},{6,14},{7,15},{16,24},{17,... | collective-permute-start | bytes 6291464 | tf_op jit(solution)/shard_map/ppermute | solution.py:466
  110.4 53.1 %copy-start = (bf16[128,64,128]{2,1,0:T(8,128)(2,1)S(1)}, bf16[128,64,128]{2,1,0:T(8,128)(2,1)}, u32[]{:S(2)}) copy-start(bf16[128,64,128]{2,1,0:T(8,128)(2,1)} %get-tuple-element.18.g_ref) | copy-start | bytes 6291460
  139.2 24.3 %collective-permute-start.1 = (bf16[128,64,128]{2,1,0:T(8,128)(2,1)}, bf16[128,64,128]{2,1,0:T(8,128)(2,1)}, u32[]{:S(2)}, u32[]{:S(2)}) collective-permute-start(bf16[128,64,128]{2,1,0:T(8,128)(2,1)} %get-tuple-element.19.refs_7_), channel_id=1, source_target_pairs={{8,0},{9,1},{10,2},{11,3},{12,4},{13,5},{14,6},{15,7},{24,16},{25,... | collective-permute-start | bytes 6291464 | tf_op jit(solution)/shard_map/ppermute | solution.py:473
  279.7 2.1 copy-start.3
  281.8 2.3 copy-start.2

commit v4 on v3

--- a/solution.py
+++ b/solution.py
@@ -145,37 +145,18 @@
     return (g_ref[r].astype(F32) + recip * (gn[r] - q * inner)).astype(BF)
 
 
-def backward_into(cols, a_ref, g_ref, w_ref, fa, fb, gh, gg, gu, gn, gin_ref):
-    rows, blk, tokens = a_ref.shape
-    recip = norm_scale(a_ref)
-    spread_back(cols, g_ref, w_ref, fa, fb, gh, gg, gu)
-    acc = back_sums(cols, a_ref, recip, w_ref, gg, gu, gn, 0, rows, jnp.zeros((8, tokens), F32))
-    inner = total_rows(acc) / (rows * blk)
-
-    def finish(r):
-        gin_ref[r] = grad_rows(a_ref, g_ref, recip, gn, inner, r)
-
-    looped(rows, 4, finish)
-
-
 def first_kernel(cols, sec, a_ref, w_ref, out_ref, xn, pg, pu, hid):
     @pl.when(sec[0] < sec[1] - 1)
     def _():
         forward_into(cols, a_ref, w_ref, out_ref, xn, pg, pu, hid)
 
 
-def middle_kernel(cols, sec, a_ref, g_ref, w_ref, out_ref, gin_ref, fa, fb, hid, xn, pg, pu, ga, gb, gn):
+def middle_kernel(cols, sec, a_ref, g_ref, w_ref, out_ref, fa, fb, hid, xn, pg, pu):
     forward_into(cols, a_ref, w_ref, out_ref, xn, pg, pu, hid, fa, fb)
 
     @pl.when(sec[0] == sec[1] - 1)
     def _():
-        backward_into(cols, a_ref, g_ref, w_ref, fa, fb, pg, ga, gb, gn, gin_ref)
-
-        def keep_grads(c):
-            fa[c] = ga[c]
-            fb[c] = gb[c]
-
-        looped(NBC, 4, keep_grads)
+        spread_back(cols, g_ref, w_ref, fa, fb, pg, fa, fb)
 
 
 def terms_at(cols, a_ref, g_ref, recip, gg, gu, hid, wg_ref, r):
@@ -190,14 +171,6 @@
 
 
 def last_kernel(cols, sec, g_ref, w_ref, fa, fb, gg, gu, gh):
-    @pl.when(sec[0] == sec[1] - 1)
-    def _():
-        def keep(c):
-            gg[c] = fa[c]
-            gu[c] = fb[c]
-
-        looped(NBC, 4, keep)
-
     @pl.when(sec[0] < sec[1] - 1)
     def _():
         spread_back(cols, g_ref, w_ref, fa, fb, gh, gg, gu)
@@ -306,20 +279,59 @@
         c.wait()
 
 
-def reduce_kernel(
-    n, sections, cols, a_ref, g_ref, w_ref, gg, gu, hid, gin_old, out_t, sums, out_ref, gin_ref,
-    terms, gn, part, near, mid, far, ys, yr, zs, zr
+def flip(dst, rows_of, pairs):
+    def body(p, carry):
+        lanes = pl.ds(pl.multiple_of(p * 2 * BLK, 2 * BLK), 2 * BLK)
+        dst[:, lanes] = jnp.concatenate([rows_of(2 * p), rows_of(2 * p + 1)], axis=0).T
+        return carry
+
+    lax.fori_loop(0, pairs, body, 0)
+
+
+def hand_copy(gin_pass, sems, other):
+    return remote(gin_pass, gin_pass, sems.at[0], sems.at[1], other)
+
+
+def upper_kernel(n, sections, cols, a_ref, g_ref, w_ref, gg, gu, hid, out_t, sums, gin_ref, out_ref, gin_pass, *scratch):
+    sec = lax.axis_index("section")
+    other = {"section": sections - 1 - sec}
+    hand = scratch[-1]
+    pairs = a_ref.shape[0] // 2
+
+    @pl.when(sec == sections - 1)
+    def _():
+        reduce_body(
+            n, cols, a_ref, g_ref, w_ref, gg, gu, hid, sums, gin_ref, *scratch[:-1],
+            upper=(out_t, out_ref, gin_pass, hand, other),
+        )
+
+    @pl.when(sec < sections - 1)
+    def _():
+        greet([other])
+        flip(out_ref, lambda r: out_t[r], pairs)
+        hand_copy(gin_pass, hand, other).wait_recv()
+
+
+def lower_kernel(n, sections, cols, a_ref, g_ref, w_ref, gg, gu, hid, sums, gin_ref, *scratch):
+    @pl.when(lax.axis_index("section") < sections - 1)
+    def _():
+        reduce_body(n, cols, a_ref, g_ref, w_ref, gg, gu, hid, sums, gin_ref, *scratch)
+
+
+def reduce_body(
+    n, cols, a_ref, g_ref, w_ref, gg, gu, hid, sums, gin_ref,
+    terms, gn, near, mid, far, ys, yr, zs, zr, upper=None
 ):
     me, partner, half, low, mine = places(n)
-    sec = lax.axis_index("section")
     rows, blk, tokens = a_ref.shape
     r_own = sums.shape[1]
-    greet([{"zero": lax.rem(mine + d, half) * 2 + low} for d in range(1, half)] + [{"zero": partner}])
+    peers = [{"zero": lax.rem(mine + d, half) * 2 + low} for d in range(1, half)]
+    greet(peers + [{"zero": partner}] + ([upper[-1]] if upper else []))
     order = list(range(1, half)) + [0]
     todo = len(order)
     sent = []
     recip = norm_scale(a_ref)
-    part[...] = jnp.zeros_like(part)
+    part = jnp.zeros((8, tokens), F32)
 
     def position(d):
         return lax.rem(mine + d, half) * 2
@@ -330,7 +342,19 @@
 
         looped(r_own, 4, body)
 
-    for d in order:
+    for i, d in enumerate(order):
+        if i == 2 and upper:
+            part = back_sums(cols, a_ref, recip, w_ref, gg, gu, gn, 0, rows, part)
+            inner = total_rows(part) / (rows * blk)
+            out_t, out_ref, gin_pass, hand, other = upper
+
+            def finish(r):
+                gin_pass[r] = grad_rows(a_ref, g_ref, recip, gn, inner, r)
+
+            looped(rows, 4, finish)
+            c = hand_copy(gin_pass, hand, other)
+            c.start()
+            sent.append(c)
         who = position(d) + 1 - low
         block_of(who)
         for m in range(3):
@@ -341,12 +365,9 @@
 
     for i, d in enumerate(order):
         block_of(position(d) + low)
-
-        @pl.when(sec < sections - 1)
-        def _():
+        if not upper:
             first, last = (i * rows // todo, (i + 1) * rows // todo)
-            part[...] = back_sums(cols, a_ref, recip, w_ref, gg, gu, gn, first, last, part[...])
-
+            part = back_sums(cols, a_ref, recip, w_ref, gg, gu, gn, first, last, part)
         for m in range(3):
             remote(near.at[d, m], near.at[d, m], ys.at[d, m], yr.at[d, m], {"zero": partner}).wait_recv()
             first = (position(d) + low) * r_own
@@ -365,24 +386,13 @@
                 c.start()
                 sent.append(c)
 
-    def flipped(dst, rows_of):
-        def body(p, carry):
-            lanes = pl.ds(pl.multiple_of(p * 2 * BLK, 2 * BLK), 2 * BLK)
-            dst[:, lanes] = jnp.concatenate([rows_of(2 * p), rows_of(2 * p + 1)], axis=0).T
-            return carry
-
-        lax.fori_loop(0, rows // 2, body, 0)
-
-    flipped(out_ref, lambda r: out_t[r])
-
-    @pl.when(sec == sections - 1)
-    def _():
-        flipped(gin_ref, lambda r: gin_old[r])
-
-    @pl.when(sec < sections - 1)
-    def _():
-        inner = total_rows(part[...]) / (rows * blk)
-        flipped(gin_ref, lambda r: grad_rows(a_ref, g_ref, recip, gn, inner, r))
+    if upper:
+        out_t, out_ref, gin_pass, hand, other = upper
+        flip(out_ref, lambda r: out_t[r], rows // 2)
+        flip(gin_ref, lambda r: gin_pass[r], rows // 2)
+    else:
+        inner = total_rows(part) / (rows * blk)
+        flip(gin_ref, lambda r: grad_rows(a_ref, g_ref, recip, gn, inner, r), rows // 2)
 
     for m in range(3):
         for d in range(1, half):
@@ -420,26 +430,29 @@
     )(own, x, c)
 
 
-def reduce_all(n, sections, own_rows, cols, a, g, mats, gg, gu, hid, gin_old, out_t):
+def reduce_all(kernel, ident, n, sections, own_rows, cols, a, g, mats, gg, gu, hid, out_t=None):
     three, rows, blk, two = mats.shape
     half = n // 2
-    tokens = out_t.shape[2]
+    tokens = a.shape[2]
     flat = jax.ShapeDtypeStruct((tokens, rows * blk), BF)
     held = pltpu.VMEM((half, 3, own_rows, blk, two), BF)
     sems = pltpu.SemaphoreType.DMA((half, 3))
+    outs = [jax.ShapeDtypeStruct((three, own_rows, blk, two), F32), flat]
+    arrays = [a, g, mats, gg, gu, hid]
+    scratch = [pltpu.VMEM(mats.shape, BF), pltpu.VMEM((rows, blk, tokens), F32)]
+    scratch += [held, held, held, sems, sems, sems, sems]
+    if out_t is not None:
+        outs += [flat, jax.ShapeDtypeStruct(a.shape, BF)]
+        arrays += [out_t]
+        scratch += [pltpu.SemaphoreType.DMA((2,))]
     return pl.pallas_call(
-        lambda *refs: reduce_kernel(n, sections, *refs),
-        out_shape=[jax.ShapeDtypeStruct((three, own_rows, blk, two), F32), flat, flat],
-        in_specs=[pl.BlockSpec(memory_space=pltpu.SMEM)] + [VMEM] * 8,
-        out_specs=[VMEM] * 3,
-        scratch_shapes=[
-            pltpu.VMEM(mats.shape, BF),
-            pltpu.VMEM((rows, blk, tokens), F32),
-            pltpu.VMEM((8, tokens), F32),
-            held, held, held, sems, sems, sems, sems,
-        ],
-        compiler_params=pltpu.CompilerParams(collective_id=1, has_side_effects=True, vmem_limit_bytes=LIMIT),
-    )(cols, a, g, mats, gg, gu, hid, gin_old, out_t)
+        lambda *refs: kernel(n, sections, *refs),
+        out_shape=outs,
+        in_specs=[pl.BlockSpec(memory_space=pltpu.SMEM)] + [VMEM] * len(arrays),
+        out_specs=[VMEM] * len(outs),
+        scratch_shapes=scratch,
+        compiler_params=pltpu.CompilerParams(collective_id=ident, has_side_effects=True, vmem_limit_bytes=LIMIT),
+    )(cols, *arrays)
 
 
 def shards(inputs, cotangent, weights, keep, columns):
@@ -465,19 +478,23 @@
     )
     moved = lax.ppermute(out, "section", [(0, 1)])
     current = jnp.where(section_id == 0, start, moved)
-    out, gin, fa, fb, hid = call(
+    out, fa, fb, hid = call(
         middle_kernel, cols, sec, (current, cot, mats),
-        [(tall, BF), (tall, BF), (wide, BF), (wide, BF), (wide, BF)],
-        [(tall, BF), (wide, F32), (wide, F32), (wide, BF), (wide, BF), (tall, F32)],
-    )
-    moved = lax.ppermute(gin, "section", [(1, 0)])
-    upstream = jnp.where(section_id == sections - 1, cot, moved)
+        [(tall, BF), (wide, BF), (wide, BF), (wide, BF)],
+        [(tall, BF), (wide, F32), (wide, F32)],
+    )
+    is_upper = section_id == sections - 1
+    sums_upper, gin_upper, out, upstream = reduce_all(
+        upper_kernel, 1, n, sections, own_rows, cols, current, cot, mats, fa, fb, hid, out
+    )
     gg, gu = call(
         last_kernel, cols, sec, (upstream, mats, fa, fb), [(wide, BF), (wide, BF)], [(wide, F32)]
     )
-    summed, out, gin = reduce_all(
-        n, sections, own_rows, cols, current, upstream, mats, gg, gu, hid, gin, out
-    )
+    sums_lower, gin_lower = reduce_all(
+        lower_kernel, 2, n, sections, own_rows, cols, current, upstream, mats, gg, gu, hid
+    )
+    summed = jnp.where(is_upper, sums_upper, sums_lower)
+    gin = jnp.where(is_upper, gin_upper, gin_lower)
     grad = summed.reshape(3, own_rows, BLK, 2, BLK).transpose(0, 1, 3, 2, 4)
     grad = grad.reshape(3, own_rows, 2, BLK * BLK)
     grad = grad * own_keep[..., None].astype(F32) * norm_factor

time: 286 us -> 269 us (0.941)
  waiting for transfers between devices: 25.7 us -> 2.64 us
  Pallas kernels: 220 us -> 226 us
  other arithmetic: 10.2 us -> 13.1 us
    ppermute x1 -> x0, waiting for transfers between devices: 22.9 us -> none  [shards(): moved = lax.ppermute(gin, 'section', [(1, 0)])]
    pallas_call x1 -> x2, Pallas kernels: 88 us -> 95.6 us  [reduce_all(): pl.pallas_call(lambda *refs: kernel(n, sections, *refs), out_shape=outs,...]
    broadcast_in_dim x0 -> x1, other arithmetic: none -> 3.28 us  [shards(): return (out[None], gin[None], grad[None])]
  transfers between devices with their start and end apart: 2 -> 1, of which waited for: 2 -> 1; matrix products, arithmetic and copies ran while one was open for 0% -> 0% of each run, Pallas kernels for 0% -> 0%
where the time goes in v4:
time: 269 us
  Pallas kernels  226 us (84%)
  local copies, waits for them, and re-layouts  15.4 us (6%)
  other arithmetic  13.1 us (5%)
  starting transfers between devices  10.2 us (4%)
    pallas_call x2, Pallas kernels, reduce_all(): pl.pallas_call(lambda *refs: kernel(n, sections, *refs), out_shape=outs,...  95.6 us
    pallas_call x3, Pallas kernels, call(): pl.pallas_call(kernel, out_shape=[jax.ShapeDtypeStruct(s, d) for s, d in...  68.1 us
    pallas_call x1, Pallas kernels, gather_all(): pl.pallas_call(lambda *refs: gather_kernel(n, sections, *refs), out_shape...  62.7 us
    ppermute x1, starting transfers between devices, shards(): moved = lax.ppermute(out, 'section', [(0, 1)])  10.2 us
  transfers between devices with their start and end apart: 1, of which 1 were waited for; matrix products, arithmetic and copies ran while one was open for 0% of the time, Pallas kernels for 0%

profile of v4, /device:TPU:0, one launch (start us, length us, event | category | flops | bytes accessed | tf_op | source)
XLA Modules:
  0.0 268.5 jit_solution(3700789827399058526)
XLA Ops:
  0.6 0.8 convert_bitcast_fusion
  1.4 0.1 copy.13
  1.5 3.0 %squeeze.3 = bf16[3,16,2,64,64]{4,3,2,1,0:T(8,128)(2,1)S(1)} reshape(bf16[1,3,16,2,4096]{4,3,2,1,0:T(2,128)(2,1)} %param.7) | data formatting | bytes 1572864 | tf_op jit(solution)/shard_map/squeeze | solution.py:467
  4.5 0.0 copy-start.4
  4.5 1.9 fusion
  6.4 1.5 reshape.46.refs_0_
  7.9 0.0 copy-done.4
  7.9 0.1 copy.12
  8.0 0.7 reshape_squeeze.3.cols.refs_0_
  8.8 0.6 pad_add_fusion.sec
  9.4 62.7 %shard_map.76 = (bf16[3,128,64,128]{3,2,1,0:T(8,128)(2,1)}, bf16[128,64,128]{2,1,0:T(8,128)(2,1)}, bf16[128,64,128]{2,1,0:T(8,128)(2,1)}) custom-call(bf16[3,16,64,128]{3,2,1,0:T(8,128)(2,1)} %reshape.46.refs_0_, bf16[128,8192]{1,0:T(8,128)(2,1)} %refs_1_.1, bf16[128,8192]{1,0:T(8,128)(2,1)} %refs_2_.1), custom_call_target="tpu_custom_call" | custom-call | tf_op jit(solution)/shard_map/pallas_call | solution.py:419
  72.1 0.0 copy-start
  72.1 23.7 %shard_map.77 = bf16[128,64,128]{2,1,0:T(8,128)(2,1)} custom-call(s32[768]{0:T(1024)} %reshape_squeeze.3.cols.refs_0_, s32[2]{0:T(128)} %pad_add_fusion.sec, bf16[128,64,128]{2,1,0:T(8,128)(2,1)} %get-tuple-element.18.a_ref, bf16[3,128,64,128]{3,2,1,0:T(8,128)(2,1)} %get-tuple-element.19.w_ref.refs_3_), custom_call_target="tpu_custom_call" | custom-call | tf_op jit(solution)/shard_map/pallas_call | solution.py:185
  95.8 10.2 %collective-permute-start = (bf16[128,64,128]{2,1,0:T(8,128)(2,1)}, bf16[128,64,128]{2,1,0:T(8,128)(2,1)}, u32[]{:S(2)}, u32[]{:S(2)}) collective-permute-start(bf16[128,64,128]{2,1,0:T(8,128)(2,1)} %shard_map.77), channel_id=1, source_target_pairs={{0,8},{1,9},{2,10},{3,11},{4,12},{5,13},{6,14},{7,15},{16,24},{17,... | collective-permute-start | bytes 6291464 | tf_op jit(solution)/shard_map/ppermute | solution.py:479
  106.0 0.1 copy.16
  106.1 2.6 collective-permute-done
  108.7 0.0 copy-done
  108.8 1.5 broadcast_select_fusion.a_ref.refs_1_
  110.3 28.1 %shard_map.78 = (bf16[128,64,128]{2,1,0:T(8,128)(2,1)}, bf16[172,64,128]{2,1,0:T(8,128)(2,1)}, bf16[172,64,128]{2,1,0:T(8,128)(2,1)}, bf16[172,64,128]{2,1,0:T(8,128)(2,1)}) custom-call(s32[768]{0:T(1024)} %reshape_squeeze.3.cols.refs_0_, s32[2]{0:T(128)} %pad_add_fusion.sec, bf16[128,64,128]{2,1,0:T(8,128)(2,1)} %broadcast_select_fusion.a_ref.refs_1_, ...), custom_call_target="tpu_custom_call" | custom-call | tf_op jit(solution)/shard_map/pallas_call | solution.py:185
  138.4 41.8 %shard_map.79 = (f32[3,16,64,128]{3,2,1,0:T(8,128)}, bf16[128,8192]{1,0:T(8,128)(2,1)}, bf16[128,8192]{1,0:T(8,128)(2,1)}, bf16[128,64,128]{2,1,0:T(8,128)(2,1)}) custom-call(s32[768]{0:T(1024)} %reshape_squeeze.3.cols.refs_0_, bf16[128,64,128]{2,1,0:T(8,128)(2,1)} %broadcast_select_fusion.a_ref.refs_1_, ...), custom_call_target="tpu_custom_call" | custom-call | tf_op jit(solution)/shard_map/pallas_call | solution.py:448
  180.1 16.3 %shard_map.80 = (bf16[172,64,128]{2,1,0:T(8,128)(2,1)}, bf16[172,64,128]{2,1,0:T(8,128)(2,1)}) custom-call(s32[768]{0:T(1024)} %reshape_squeeze.3.cols.refs_0_, s32[2]{0:T(128)} %pad_add_fusion.sec, bf16[128,64,128]{2,1,0:T(8,128)(2,1)} %get-tuple-element.27.g_ref.refs_2_, bf16[3,128,64,128]{3,2,1,0:T(8,128)(2,1)} %get-tuple-element.19.w_ref.refs_3_, ...), custom_call_target="tpu_custom_call" | custom-call | tf_op jit(solution)/shard_map/pallas_call | solution.py:185
  196.5 53.9 %shard_map.81 = (f32[3,16,64,128]{3,2,1,0:T(8,128)}, bf16[128,8192]{1,0:T(8,128)(2,1)}) custom-call(s32[768]{0:T(1024)} %reshape_squeeze.3.cols.refs_0_, bf16[128,64,128]{2,1,0:T(8,128)(2,1)} %broadcast_select_fusion.a_ref.refs_1_, bf16[128,64,128]{2,1,0:T(8,128)(2,1)} %get-tuple-element.27.g_ref.refs_2_, ...), custom_call_target="tpu_custom_call" | custom-call | tf_op jit(solution)/shard_map/pallas_call | solution.py:448
  250.3 0.0 copy-done.3
  250.4 2.9 %broadcast_select_fusion.1 = f32[3,16,64,128]{3,2,1,0:T(8,128)} fusion(f32[3,16,64,128]{3,2,1,0:T(8,128)S(1)} %copy-done.3, f32[3,16,64,128]{3,2,1,0:T(8,128)} %get-tuple-element.32, pred[]{:T(512)S(6)} %eq.7), kind=kLoop, calls=%fused_computation.5 | loop fusion | flops 393216 | bytes 4718593 | tf_op jit(solution)/shard_map/jit(_where)/select_n | solution.py:496
  253.3 3.2 %reshape.47 = f32[3,16,64,2,64]{4,3,2,1,0:T(2,128)S(1)} reshape(f32[3,16,64,128]{3,2,1,0:T(8,128)} %broadcast_select_fusion.1) | data formatting | bytes 3145728 | tf_op jit(solution)/shard_map/reshape | solution.py:498
  256.5 2.1 copy.15
  258.6 3.3 %reshape.48 = f32[1,3,16,2,4096]{4,3,2,1,0:T(2,128)S(1)} reshape(f32[3,16,2,64,64]{4,3,2,1,0:T(8,128)} %copy.15) | data formatting | bytes 3145728 | tf_op jit(solution)/shard_map/reshape | solution.py:499
  261.8 2.1 multiply_multiply_fusion
  263.9 0.0 copy-done.1
  263.9 3.3 %select_bitcast_fusion = bf16[1,128,8192]{2,1,0:T(8,128)(2,1)} fusion(bf16[128,8192]{1,0:T(8,128)(2,1)S(1)} %copy-done.1, bf16[128,8192]{1,0:T(8,128)(2,1)} %get-tuple-element.30, pred[]{:T(512)S(6)} %eq.7), kind=kLoop, calls=%fused_computation | loop fusion | flops 1048576 | bytes 6291457 | tf_op jit(solution)/shard_map/broadcast_in_dim | solution.py:501
  267.2 0.0 copy-done.2
  267.2 1.3 copy.21
  (3 shorter events, 0.0 us)
Async XLA Ops:
  4.5 3.4 %copy-start.4 = (s32[1,3,128,2]{2,3,1,0:T(2,128)S(1)}, s32[1,3,128,2]{2,3,1,0:T(2,128)}, u32[]{:S(2)}) copy-start(s32[1,3,128,2]{2,3,1,0:T(2,128)} %param.9) | copy-start | bytes 9220
  72.1 36.6 %copy-start = (bf16[128,64,128]{2,1,0:T(8,128)(2,1)S(1)}, bf16[128,64,128]{2,1,0:T(8,128)(2,1)}, u32[]{:S(2)}) copy-start(bf16[128,64,128]{2,1,0:T(8,128)(2,1)} %get-tuple-element.18.a_ref) | copy-start | bytes 6291460
  95.8 12.9 %collective-permute-start = (bf16[128,64,128]{2,1,0:T(8,128)(2,1)}, bf16[128,64,128]{2,1,0:T(8,128)(2,1)}, u32[]{:S(2)}, u32[]{:S(2)}) collective-permute-start(bf16[128,64,128]{2,1,0:T(8,128)(2,1)} %shard_map.77), channel_id=1, source_target_pairs={{0,8},{1,9},{2,10},{3,11},{4,12},{5,13},{6,14},{7,15},{16,24},{17,... | collective-permute-start | bytes 6291464 | tf_op jit(solution)/shard_map/ppermute | solution.py:479
  196.5 53.9 %copy-start.3 = (f32[3,16,64,128]{3,2,1,0:T(8,128)S(1)}, f32[3,16,64,128]{3,2,1,0:T(8,128)}, u32[]{:S(2)}) copy-start(f32[3,16,64,128]{3,2,1,0:T(8,128)} %get-tuple-element.31) | copy-start | bytes 4718596
  261.8 2.1 copy-start.1
  263.9 3.3 %copy-start.2 = (bf16[128,8192]{1,0:T(8,128)(2,1)S(1)}, bf16[128,8192]{1,0:T(8,128)(2,1)}, u32[]{:S(2)}) copy-start(bf16[128,8192]{1,0:T(8,128)(2,1)} %get-tuple-element.25) | copy-start | bytes 6291460

commit v5 on v4

--- a/solution.py
+++ b/solution.py
@@ -343,7 +343,7 @@
         looped(r_own, 4, body)
 
     for i, d in enumerate(order):
-        if i == 2 and upper:
+        if i == 1 and upper:
             part = back_sums(cols, a_ref, recip, w_ref, gg, gu, gn, 0, rows, part)
             inner = total_rows(part) / (rows * blk)
             out_t, out_ref, gin_pass, hand, other = upper

time: 269 us -> 268 us (level)
  no operation moved by 1% of the time
where the time goes in v5:
time: 268 us; the launch traced here: 267 us
  Pallas kernels  225 us (84%)
  local copies, waits for them, and re-layouts  15.4 us (6%)
  other arithmetic  13.1 us (5%)
  starting transfers between devices  10.2 us (4%)
    pallas_call x2, Pallas kernels, reduce_all(): pl.pallas_call(lambda *refs: kernel(n, sections, *refs), out_shape=outs,...  94.4 us
    pallas_call x3, Pallas kernels, call(): pl.pallas_call(kernel, out_shape=[jax.ShapeDtypeStruct(s, d) for s, d in...  68.1 us
    pallas_call x1, Pallas kernels, gather_all(): pl.pallas_call(lambda *refs: gather_kernel(n, sections, *refs), out_shape...  62.7 us
    ppermute x1, starting transfers between devices, shards(): moved = lax.ppermute(out, 'section', [(0, 1)])  10.2 us
  transfers between devices with their start and end apart: 1, of which 1 were waited for; matrix products, arithmetic and copies ran while one was open for 0% of the time, Pallas kernels for 0%

profile of v5, /device:TPU:0, one launch (start us, length us, event | category | flops | bytes accessed | tf_op | source)
XLA Modules:
  0.0 267.3 jit_solution(4233849255368502321)
XLA Ops:
  0.6 0.8 convert_bitcast_fusion
  1.4 0.1 copy.13
  1.5 3.0 %squeeze.3 = bf16[3,16,2,64,64]{4,3,2,1,0:T(8,128)(2,1)S(1)} reshape(bf16[1,3,16,2,4096]{4,3,2,1,0:T(2,128)(2,1)} %param.7) | data formatting | bytes 1572864 | tf_op jit(solution)/shard_map/squeeze | solution.py:467
  4.5 0.0 copy-start.4
  4.5 1.9 fusion
  6.4 1.5 reshape.46.refs_0_
  7.9 0.0 copy-done.4
  7.9 0.1 copy.12
  8.0 0.7 reshape_squeeze.3.cols.refs_0_
  8.8 0.6 pad_add_fusion.sec
  9.4 62.7 %shard_map.76 = (bf16[3,128,64,128]{3,2,1,0:T(8,128)(2,1)}, bf16[128,64,128]{2,1,0:T(8,128)(2,1)}, bf16[128,64,128]{2,1,0:T(8,128)(2,1)}) custom-call(bf16[3,16,64,128]{3,2,1,0:T(8,128)(2,1)} %reshape.46.refs_0_, bf16[128,8192]{1,0:T(8,128)(2,1)} %refs_1_.1, bf16[128,8192]{1,0:T(8,128)(2,1)} %refs_2_.1), custom_call_target="tpu_custom_call" | custom-call | tf_op jit(solution)/shard_map/pallas_call | solution.py:419
  72.1 0.0 copy-start
  72.1 23.7 %shard_map.77 = bf16[128,64,128]{2,1,0:T(8,128)(2,1)} custom-call(s32[768]{0:T(1024)} %reshape_squeeze.3.cols.refs_0_, s32[2]{0:T(128)} %pad_add_fusion.sec, bf16[128,64,128]{2,1,0:T(8,128)(2,1)} %get-tuple-element.18.a_ref, bf16[3,128,64,128]{3,2,1,0:T(8,128)(2,1)} %get-tuple-element.19.w_ref.refs_3_), custom_call_target="tpu_custom_call" | custom-call | tf_op jit(solution)/shard_map/pallas_call | solution.py:185
  95.8 10.2 %collective-permute-start = (bf16[128,64,128]{2,1,0:T(8,128)(2,1)}, bf16[128,64,128]{2,1,0:T(8,128)(2,1)}, u32[]{:S(2)}, u32[]{:S(2)}) collective-permute-start(bf16[128,64,128]{2,1,0:T(8,128)(2,1)} %shard_map.77), channel_id=1, source_target_pairs={{0,8},{1,9},{2,10},{3,11},{4,12},{5,13},{6,14},{7,15},{16,24},{17,... | collective-permute-start | bytes 6291464 | tf_op jit(solution)/shard_map/ppermute | solution.py:479
  106.0 0.1 copy.16
  106.1 2.6 collective-permute-done
  108.7 0.0 copy-done
  108.8 1.5 broadcast_select_fusion.a_ref.refs_1_
  110.3 28.1 %shard_map.78 = (bf16[128,64,128]{2,1,0:T(8,128)(2,1)}, bf16[172,64,128]{2,1,0:T(8,128)(2,1)}, bf16[172,64,128]{2,1,0:T(8,128)(2,1)}, bf16[172,64,128]{2,1,0:T(8,128)(2,1)}) custom-call(s32[768]{0:T(1024)} %reshape_squeeze.3.cols.refs_0_, s32[2]{0:T(128)} %pad_add_fusion.sec, bf16[128,64,128]{2,1,0:T(8,128)(2,1)} %broadcast_select_fusion.a_ref.refs_1_, ...), custom_call_target="tpu_custom_call" | custom-call | tf_op jit(solution)/shard_map/pallas_call | solution.py:185
  138.4 40.6 %shard_map.79 = (f32[3,16,64,128]{3,2,1,0:T(8,128)}, bf16[128,8192]{1,0:T(8,128)(2,1)}, bf16[128,8192]{1,0:T(8,128)(2,1)}, bf16[128,64,128]{2,1,0:T(8,128)(2,1)}) custom-call(s32[768]{0:T(1024)} %reshape_squeeze.3.cols.refs_0_, bf16[128,64,128]{2,1,0:T(8,128)(2,1)} %broadcast_select_fusion.a_ref.refs_1_, ...), custom_call_target="tpu_custom_call" | custom-call | tf_op jit(solution)/shard_map/pallas_call | solution.py:448
  178.9 16.3 %shard_map.80 = (bf16[172,64,128]{2,1,0:T(8,128)(2,1)}, bf16[172,64,128]{2,1,0:T(8,128)(2,1)}) custom-call(s32[768]{0:T(1024)} %reshape_squeeze.3.cols.refs_0_, s32[2]{0:T(128)} %pad_add_fusion.sec, bf16[128,64,128]{2,1,0:T(8,128)(2,1)} %get-tuple-element.27.g_ref.refs_2_, bf16[3,128,64,128]{3,2,1,0:T(8,128)(2,1)} %get-tuple-element.19.w_ref.refs_3_, ...), custom_call_target="tpu_custom_call" | custom-call | tf_op jit(solution)/shard_map/pallas_call | solution.py:185
  195.3 53.9 %shard_map.81 = (f32[3,16,64,128]{3,2,1,0:T(8,128)}, bf16[128,8192]{1,0:T(8,128)(2,1)}) custom-call(s32[768]{0:T(1024)} %reshape_squeeze.3.cols.refs_0_, bf16[128,64,128]{2,1,0:T(8,128)(2,1)} %broadcast_select_fusion.a_ref.refs_1_, bf16[128,64,128]{2,1,0:T(8,128)(2,1)} %get-tuple-element.27.g_ref.refs_2_, ...), custom_call_target="tpu_custom_call" | custom-call | tf_op jit(solution)/shard_map/pallas_call | solution.py:448
  249.1 0.0 copy-done.3
  249.1 2.9 %broadcast_select_fusion.1 = f32[3,16,64,128]{3,2,1,0:T(8,128)} fusion(f32[3,16,64,128]{3,2,1,0:T(8,128)S(1)} %copy-done.3, f32[3,16,64,128]{3,2,1,0:T(8,128)} %get-tuple-element.32, pred[]{:T(512)S(6)} %eq.7), kind=kLoop, calls=%fused_computation.5 | loop fusion | flops 393216 | bytes 4718593 | tf_op jit(solution)/shard_map/jit(_where)/select_n | solution.py:496
  252.1 3.2 %reshape.47 = f32[3,16,64,2,64]{4,3,2,1,0:T(2,128)S(1)} reshape(f32[3,16,64,128]{3,2,1,0:T(8,128)} %broadcast_select_fusion.1) | data formatting | bytes 3145728 | tf_op jit(solution)/shard_map/reshape | solution.py:498
  255.3 2.1 copy.15
  257.4 3.3 %reshape.48 = f32[1,3,16,2,4096]{4,3,2,1,0:T(2,128)S(1)} reshape(f32[3,16,2,64,64]{4,3,2,1,0:T(8,128)} %copy.15) | data formatting | bytes 3145728 | tf_op jit(solution)/shard_map/reshape | solution.py:499
  260.6 0.0 copy-start.1
  260.6 2.1 multiply_multiply_fusion
  262.7 0.0 copy-done.1
  262.7 3.3 %select_bitcast_fusion = bf16[1,128,8192]{2,1,0:T(8,128)(2,1)} fusion(bf16[128,8192]{1,0:T(8,128)(2,1)S(1)} %copy-done.1, bf16[128,8192]{1,0:T(8,128)(2,1)} %get-tuple-element.30, pred[]{:T(512)S(6)} %eq.7), kind=kLoop, calls=%fused_computation | loop fusion | flops 1048576 | bytes 6291457 | tf_op jit(solution)/shard_map/broadcast_in_dim | solution.py:501
  266.0 1.3 copy.21
  (3 shorter events, 0.0 us)
Async XLA Ops:
  4.5 3.4 %copy-start.4 = (s32[1,3,128,2]{2,3,1,0:T(2,128)S(1)}, s32[1,3,128,2]{2,3,1,0:T(2,128)}, u32[]{:S(2)}) copy-start(s32[1,3,128,2]{2,3,1,0:T(2,128)} %param.9) | copy-start | bytes 9220
  72.1 36.6 %copy-start = (bf16[128,64,128]{2,1,0:T(8,128)(2,1)S(1)}, bf16[128,64,128]{2,1,0:T(8,128)(2,1)}, u32[]{:S(2)}) copy-start(bf16[128,64,128]{2,1,0:T(8,128)(2,1)} %get-tuple-element.18.a_ref) | copy-start | bytes 6291460
  95.8 12.9 %collective-permute-start = (bf16[128,64,128]{2,1,0:T(8,128)(2,1)}, bf16[128,64,128]{2,1,0:T(8,128)(2,1)}, u32[]{:S(2)}, u32[]{:S(2)}) collective-permute-start(bf16[128,64,128]{2,1,0:T(8,128)(2,1)} %shard_map.77), channel_id=1, source_target_pairs={{0,8},{1,9},{2,10},{3,11},{4,12},{5,13},{6,14},{7,15},{16,24},{17,... | collective-permute-start | bytes 6291464 | tf_op jit(solution)/shard_map/ppermute | solution.py:479
  195.3 53.9 %copy-start.3 = (f32[3,16,64,128]{3,2,1,0:T(8,128)S(1)}, f32[3,16,64,128]{3,2,1,0:T(8,128)}, u32[]{:S(2)}) copy-start(f32[3,16,64,128]{3,2,1,0:T(8,128)} %get-tuple-element.31) | copy-start | bytes 4718596
  260.6 2.1 copy-start.1
  262.7 3.3 %copy-start.2 = (bf16[128,8192]{1,0:T(8,128)(2,1)S(1)}, bf16[128,8192]{1,0:T(8,128)(2,1)}, u32[]{:S(2)}) copy-start(bf16[128,8192]{1,0:T(8,128)(2,1)} %get-tuple-element.25) | copy-start | bytes 6291460
